TPU v7x, 512 devices: a whole 4x8x8 slice. The times are simulated.
512 devices in a mesh: freq: 8 (over x, z_hi), slab: 64 (over y, z_lo, core).
Axes of the slice: x: 4, y: 8, z: 8 (z_hi: 2, z_lo: 4; z = z_hi * 4 + z_lo), core: 2. Of those that a mesh axis runs over, the one named last changes fastest.
Arguments:
- wavefield: float32 [8, 2, 2, 1024, 2048], P('freq', None, None, 'slab'), may hold values from -6 to 6
- velocity: float32 [2, 1024, 2048], P(None, 'slab', 'freq'), may hold values from 1500 to 4500
- reference_velocity: float32 [2], replicated, may hold values from 1400 to 2200
- frequencies: float32 [8], P('freq'), may hold values from 5 to 40
- block_x: float32 [8, 2, 128, 128], P('freq'), may hold values from -0.125 to 0.125
- block_y: float32 [8, 2, 128, 128], P('freq'), may hold values from -0.125 to 0.125
Outputs:
- propagated: float32 [8, 2, 2, 1024, 2048], P('freq', None, None, 'slab')
- images: float32 [2, 1024, 2048], P(None, 'slab')
All inputs are finite; a program needn't handle non-finite values.
Results may differ from a plain program's by a relative error of at most 0.0003.
Values sent between devices are 32-bit elements; how exact they have to be, the bound alone decides.
A program may use at most 64 MiB of HBM per device.

v0:
```python
import math

import jax
import jax.numpy as jnp
from jax import lax
from jax.sharding import PartitionSpec as P

DEPTHS = 2


spacing = 12.5
depth_step = 10.0
inner_length = 128


def contract(formula, left, right):
    return jnp.einsum(formula, left, right, precision=lax.Precision.HIGHEST)


def rotate(values, factor_real, factor_imag):
    trailing = values.ndim - 3
    signs = jnp.array([-1.0, 1.0], dtype=jnp.float32).reshape((2,) + (1,) * trailing)
    return values * factor_real + jnp.flip(values, axis=2) * (factor_imag * signs)


def angle_table(rows_index, cols_index, period, direction):
    product = rows_index[:, None] * cols_index[None, :] % period
    angles = direction * 2.0 * math.pi * product.astype(jnp.float32) / period
    return (jnp.cos(angles), jnp.sin(angles))


def block_table(cos_part, sin_part):
    return jnp.stack((jnp.stack((cos_part, sin_part)), jnp.stack((-sin_part, cos_part))))


def line_transform(fields, direction):
    length = fields.shape[-1]
    outer = length // inner_length
    outer_index = jnp.arange(outer, dtype=jnp.int32)
    inner_index = jnp.arange(inner_length, dtype=jnp.int32)
    first_table = block_table(*angle_table(outer_index, outer_index, outer, direction))
    twist_cos, twist_sin = angle_table(outer_index, inner_index, length, direction)
    second_table = block_table(*angle_table(inner_index, inner_index, inner_length, direction))
    flat_shape = fields.shape
    tiled = fields.reshape(flat_shape[:4] + (outer, inner_length))
    if direction < 0:
        tiled = contract("fgcrab,cdak->fgdrkb", tiled, first_table)
        tiled = rotate(tiled, twist_cos, twist_sin)
        tiled = contract("fgcrkb,cdbm->fgdrkm", tiled, second_table)
        return tiled.reshape(flat_shape)
    tiled = contract("fgcrkm,cdmb->fgdrkb", tiled, second_table)
    tiled = rotate(tiled, twist_cos, twist_sin)
    tiled = contract("fgcrkb,cdka->fgdrab", tiled, first_table)
    return tiled.reshape(flat_shape) * (1.0 / length)


def spectral_wavenumber(positions, length):
    outer = length // inner_length
    leading = positions // inner_length
    trailing = positions % inner_length
    frequency_index = leading + outer * trailing
    signed = jnp.where(frequency_index >= length // 2, frequency_index - length, frequency_index)
    return 2.0 * math.pi * signed.astype(jnp.float32) / (length * spacing)


def phase_shift(fields, angular, ref_speed, slab_index):
    row_count = fields.shape[3]
    length = fields.shape[4]
    slab_count = lax.axis_size("slab")
    last_numbers = spectral_wavenumber(jnp.arange(length, dtype=jnp.int32), length)
    row_positions = slab_index * row_count + jnp.arange(row_count, dtype=jnp.int32)
    row_numbers = spectral_wavenumber(row_positions, row_count * slab_count)
    vertical = (
        (angular[:, None, None] / ref_speed) ** 2
        - last_numbers[None, None, :] ** 2
        - row_numbers[None, :, None] ** 2
    )
    magnitude = jnp.sqrt(jnp.abs(vertical))
    travels = vertical >= 0
    factor_real = jnp.where(
        travels, jnp.cos(depth_step * magnitude), jnp.exp(-depth_step * magnitude)
    )
    factor_imag = jnp.where(travels, jnp.sin(depth_step * magnitude), 0.0)
    return rotate(fields, factor_real[:, None, None], factor_imag[:, None, None])


def split_step(fields, angular, ref_speed, speed):
    angles = angular[:, None, None] * depth_step * (1.0 / speed - 1.0 / ref_speed)[None]
    return rotate(fields, jnp.cos(angles)[:, None, None], jnp.sin(angles)[:, None, None])


def second_difference(values):
    padded = jnp.pad(values, ((0, 0),) * (values.ndim - 1) + ((1, 1),))
    return padded[..., 2:] - 2.0 * values + padded[..., :-2]


def correct_lines(fields, ref_speed, speed, blocks):
    strength = 0.5 * (1.0 - ref_speed / speed)
    signs = jnp.array([-1.0, 1.0], dtype=jnp.float32).reshape((2, 1, 1))
    mixed = fields + jnp.flip(second_difference(fields), axis=2) * (strength * signs)
    size_block = blocks.shape[-1]
    tiled_shape = fields.shape[:4] + (fields.shape[4] // size_block, size_block)
    tiles = mixed.reshape(tiled_shape)
    eye_block = jnp.eye(size_block, dtype=jnp.float32)
    matrix_real = blocks[:, 0] + eye_block[None]
    matrix_imag = blocks[:, 1]
    table = jnp.stack(
        (jnp.stack((matrix_real, matrix_imag), 1), jnp.stack((-matrix_imag, matrix_real), 1)), 1
    )
    return contract("fgcrni,fcdji->fgdrnj", tiles, table).reshape(fields.shape)


def swap_lines(fields):
    exchanged = lax.all_to_all(fields, "slab", split_axis=4, concat_axis=3, tiled=True)
    return jnp.swapaxes(exchanged, 3, 4)


def local_image(fields):
    return jnp.sum(fields[:, 0, 0] * fields[:, 1, 0] - fields[:, 0, 1] * fields[:, 1, 1], axis=0)


def image_total(fields):
    return lax.psum(local_image(fields), "freq")


def body(wavefield, velocity, reference_velocity, frequencies, block_x, block_y):
    angular = 2.0 * math.pi * frequencies
    slab_index = lax.axis_index("slab")
    blocks = {"x": block_x, "y": block_y}
    fields = wavefield
    layout = "x"
    images = []
    for depth_index in range(DEPTHS):
        ref_speed = reference_velocity[depth_index]
        speed_x = lax.all_gather(
            velocity[depth_index : depth_index + 1], "freq", axis=2, tiled=True
        )[0]
        speed_y = jnp.swapaxes(
            lax.all_to_all(speed_x, "slab", split_axis=1, concat_axis=0, tiled=True), 0, 1
        )
        speeds = {"x": speed_x, "y": speed_y}
        fields = line_transform(fields, -1)
        fields = swap_lines(fields)
        fields = line_transform(fields, -1)
        fields = phase_shift(fields, angular, ref_speed, slab_index)
        fields = line_transform(fields, 1)
        fields = swap_lines(fields)
        fields = line_transform(fields, 1)
        fields = split_step(fields, angular, ref_speed, speeds[layout])
        axis_order = ("x", "y") if depth_index % 2 == 0 else ("y", "x")
        for axis_name in axis_order:
            if layout != axis_name:
                fields = swap_lines(fields)
                layout = axis_name
            fields = correct_lines(fields, ref_speed, speeds[layout], blocks[layout])
        if layout != "x":
            fields = swap_lines(fields)
            layout = "x"
        images.append(image_total(fields))
    return (fields, jnp.stack(images))


def solution(mesh):
    in_specs = (
        P("freq", None, None, "slab", None),
        P(None, "slab", "freq"),
        P(),
        P("freq"),
        P("freq", None, None, None),
        P("freq", None, None, None),
    )
    out_specs = (P("freq", None, None, "slab", None), P(None, "slab", None))
    return jax.shard_map(body, mesh=mesh, in_specs=in_specs, out_specs=out_specs, check_vma=False)
```

profile of v0, /device:TPU:8, one launch (start us, length us, event | category | flops | bytes accessed | tf_op | source)
XLA Modules:
  0.0 656.1 jit_solution(18403758240056565423)
XLA Ops:
  8.0 47.1 %all_gather.6 = f32[1,16,2048]{2,1,0:T(8,128)S(1)} all-gather(f32[1,16,256]{2,1,0:T(8,128)S(1)} %get-tuple-element.33), channel_id=1, replica_groups=mesh['freq'=8,'slab'=64] {'freq'}, dimensions={2}, use_global_device_ids=true | all-gather | bytes 147456 | tf_op jit(solution)/shard_map/all_gather | solution.py:135
  57.2 10.9 %all-to-all-start.3 = ((f32[64,1,512]{2,1,0:T(1,128)}), f32[64,1,512]{2,1,0:T(1,128)S(1)}, u32[]{:S(2)}, u32[]{:S(2)}) async-start(f32[64,1,512]{2,1,0:T(1,128)} %reshape.1326), calls=%async_computation.3 | async-start | bytes 262144 | tf_op jit(solution)/shard_map/all_to_all | solution.py:139
  72.3 44.0 %all_gather.7 = f32[1,16,2048]{2,1,0:T(8,128)S(1)} all-gather(f32[1,16,256]{2,1,0:T(8,128)S(1)} %get-tuple-element.32), channel_id=1, replica_groups=mesh['freq'=8,'slab'=64] {'freq'}, dimensions={2}, use_global_device_ids=true | all-gather | bytes 147456 | tf_op jit(solution)/shard_map/all_gather | solution.py:135
  123.8 10.6 %all-to-all-start.8 = ((f32[64,1,512]{2,1,0:T(1,128)}), f32[64,1,512]{2,1,0:T(1,128)S(1)}, u32[]{:S(2)}, u32[]{:S(2)}) async-start(f32[64,1,512]{2,1,0:T(1,128)} %reshape.1336), calls=%async_computation.8 | async-start | bytes 262144 | tf_op jit(solution)/shard_map/all_to_all | solution.py:139
  135.0 3.2 copy.344
  138.2 8.0 %reshape.1320 = f32[64,1,2048]{2,1,0:T(1,128)} reshape(f32[2048,1,2,2,16]{4,3,2,1,0:T(2,128)} %bitcast.488) | data formatting | bytes 1048576
  146.9 11.1 %all-to-all-start = ((f32[64,1,2048]{2,1,0:T(1,128)}), f32[64,1,2048]{2,1,0:T(1,128)S(1)}, u32[]{:S(2)}, u32[]{:S(2)}) async-start(f32[64,1,2048]{2,1,0:T(1,128)} %reshape.1320), calls=%async_computation | async-start | bytes 1048576 | tf_op jit(solution)/shard_map/all_to_all | solution.py:114
  168.7 6.6 %all-to-all-done = f32[64,1,2048]{2,1,0:T(1,128)S(1)} async-done(((f32[64,1,2048]{2,1,0:T(1,128)}), f32[64,1,2048]{2,1,0:T(1,128)S(1)}, u32[]{:S(2)}, u32[]{:S(2)}) %all-to-all-start) | async-done | bytes 524320 | tf_op jit(solution)/shard_map/all_to_all | solution.py:114
  175.3 1.9 reduce
  177.2 7.0 %reshape.1321 = f32[2048,1,2,2,16]{4,3,2,1,0:T(2,128)} reshape(f32[64,2048]{1,0:T(8,128)S(1)} %reduce) | data formatting | bytes 1048576
  184.2 5.4 copy.346
  196.7 2.8 reshape.1322
  199.5 6.3 all-to-all-start.1
  208.5 14.5 %all-to-all-done.1 = f32[64,1,2048]{2,1,0:T(1,128)S(1)} async-done(((f32[64,1,2048]{2,1,0:T(1,128)}), f32[64,1,2048]{2,1,0:T(1,128)S(1)}, u32[]{:S(2)}, u32[]{:S(2)}) %all-to-all-start.1) | async-done | bytes 524320 | tf_op jit(solution)/shard_map/all_to_all | solution.py:114
  232.6 3.2 copy.350
  235.8 8.0 %reshape.1324 = f32[64,1,2048]{2,1,0:T(1,128)} reshape(f32[2048,1,2,2,16]{4,3,2,1,0:T(2,128)} %bitcast.490) | data formatting | bytes 1048576
  243.8 6.2 all-to-all-start.2
  251.1 16.2 %all-to-all-done.2 = f32[64,1,2048]{2,1,0:T(1,128)S(1)} async-done(((f32[64,1,2048]{2,1,0:T(1,128)}), f32[64,1,2048]{2,1,0:T(1,128)S(1)}, u32[]{:S(2)}, u32[]{:S(2)}) %all-to-all-start.2) | async-done | bytes 524320 | tf_op jit(solution)/shard_map/all_to_all | solution.py:114
  269.2 7.0 %reshape.1325 = f32[2048,1,2,2,16]{4,3,2,1,0:T(2,128)} reshape(f32[64,2048]{1,0:T(8,128)S(1)} %reduce.4) | data formatting | bytes 1048576
  276.2 5.4 copy.352
  283.7 2.2 copy.250
  288.4 2.0 reshape.1328
  290.4 23.5 %all_to_all.170 = f32[64,1,2048]{2,1,0:T(1,128)S(1)} all-to-all(f32[64,1,2048]{2,1,0:T(1,128)S(1)} %reshape.1328), channel_id=1, replica_groups=mesh['freq'=8,'slab'=64] {'slab'}, dimensions={0} | all-to-all | bytes 1048576 | tf_op jit(solution)/shard_map/all_to_all | solution.py:114
  320.9 3.2 copy.356
  324.1 7.3 %reshape.1330 = f32[64,1,2048]{2,1,0:T(1,128)S(1)} reshape(f32[2048,1,2,2,16]{4,3,2,1,0:T(2,128)} %bitcast.492) | data formatting | bytes 1048576
  331.4 23.3 %all_to_all.171 = f32[64,1,2048]{2,1,0:T(1,128)S(1)} all-to-all(f32[64,1,2048]{2,1,0:T(1,128)S(1)} %reshape.1330), channel_id=1, replica_groups=mesh['freq'=8,'slab'=64] {'slab'}, dimensions={0} | all-to-all | bytes 1048576 | tf_op jit(solution)/shard_map/all_to_all | solution.py:114
  356.6 7.0 %reshape.1331 = f32[2048,1,2,2,16]{4,3,2,1,0:T(2,128)} reshape(f32[64,2048]{1,0:T(8,128)S(1)} %reduce.6) | data formatting | bytes 1048576
  363.6 5.4 copy.358
  376.5 2.8 reshape.1332
  379.4 6.7 %all-to-all-start.6 = ((f32[64,1,2048]{2,1,0:T(1,128)}), f32[64,1,2048]{2,1,0:T(1,128)}, u32[]{:S(2)}, u32[]{:S(2)}) async-start(f32[64,1,2048]{2,1,0:T(1,128)} %reshape.1332), calls=%async_computation.6 | async-start | bytes 1048576 | tf_op jit(solution)/shard_map/all_to_all | solution.py:114
  388.4 14.7 %all-to-all-done.6 = f32[64,1,2048]{2,1,0:T(1,128)} async-done(((f32[64,1,2048]{2,1,0:T(1,128)}), f32[64,1,2048]{2,1,0:T(1,128)}, u32[]{:S(2)}, u32[]{:S(2)}) %all-to-all-start.6) | async-done | bytes 524320 | tf_op jit(solution)/shard_map/all_to_all | solution.py:114
  403.1 3.0 reduce.7
  406.1 3.1 reshape.1333
  410.9 2.0 copy.268
  412.9 2.5 all_to_all.149
  416.8 3.2 copy.366
  420.1 20.6 %reverse.7 = f32[1,2,2,16,2048]{3,2,1,0,4:T(2,128)} reverse(f32[1,2,2,16,2048]{3,2,1,0,4:T(2,128)} %bitcast.484), dimensions={2} | reverse | bytes 1048576 | tf_op jit(solution)/shard_map/reverse.1
  440.7 7.7 %fusion.137 = f32[2048,1,2,2,16]{4,3,2,1,0:T(2,128)} fusion(f32[1,2,2,16,2048]{3,2,1,0,4:T(2,128)} %reverse.7, f32[2,16,2048]{1,0,2:T(2,128)S(1)} %copy.276, f32[1,2,2,16,2048]{3,2,1,0,4:T(2,128)} %bitcast.485, f32[16,2048]{0,1:T(8,128)} %copy.273), kind=kLoop, calls=%fused_computation.286 | loop fusion | flops 393216 | bytes 1966080
  448.4 8.0 %reshape.1334 = f32[64,1,2048]{2,1,0:T(1,128)} reshape(f32[2048,1,2,2,16]{4,3,2,1,0:T(2,128)} %fusion.137) | data formatting | bytes 1048576
  456.4 6.0 all-to-all-start.7
  463.7 16.0 %all-to-all-done.7 = f32[64,1,2048]{2,1,0:T(1,128)S(1)} async-done(((f32[64,1,2048]{2,1,0:T(1,128)}), f32[64,1,2048]{2,1,0:T(1,128)S(1)}, u32[]{:S(2)}, u32[]{:S(2)}) %all-to-all-start.7) | async-done | bytes 524320 | tf_op jit(solution)/shard_map/all_to_all | solution.py:114
  481.6 7.0 %reshape.1335 = f32[2048,1,2,2,16]{4,3,2,1,0:T(2,128)} reshape(f32[64,2048]{1,0:T(8,128)S(1)} %reduce.8) | data formatting | bytes 1048576
  488.6 5.4 copy.363
  496.7 2.2 copy.284
  501.4 2.8 reshape.1338
  504.2 6.0 all-to-all-start.9
  511.1 16.4 %all-to-all-done.9 = f32[64,1,2048]{2,1,0:T(1,128)S(1)} async-done(((f32[64,1,2048]{2,1,0:T(1,128)}), f32[64,1,2048]{2,1,0:T(1,128)S(1)}, u32[]{:S(2)}, u32[]{:S(2)}) %all-to-all-start.9) | async-done | bytes 524320 | tf_op jit(solution)/shard_map/all_to_all | solution.py:114
  536.2 111.2 %all-reduce.7.cloned.1.call-done = (f32[1,16,2048]{2,1,0:T(8,128)}, f32[1,16,2048]{2,1,0:T(8,128)}) async-done(((f32[1,16,2048]{2,1,0:T(8,128)}, f32[1,16,2048]{2,1,0:T(8,128)}), (f32[1,16,2048]{2,1,0:T(8,128)}, f32[1,16,2048]{2,1,0:T(8,128)})) %all-reduce.7.cloned.1.call-update) | async-done | bytes 262160 | tf_op jit(solution)/shard_map/psum | solution.py:123
  (261 shorter events, 91.1 us)
Async XLA Ops:
  7.2 62.7 %copy-start.56 = (f32[2]{0:T(128)S(1)}, f32[2]{0:T(128)}, u32[]{:S(2)}) copy-start(f32[2]{0:T(128)} %param.24) | copy-start | bytes 28
  7.2 109.2 %copy-start.23 = (f32[1,2,2,16,2048]{4,3,2,1,0:T(8,128)S(1)}, f32[1,2,2,16,2048]{4,3,2,1,0:T(8,128)}, u32[]{:S(2)}) copy-start(f32[1,2,2,16,2048]{4,3,2,1,0:T(8,128)} %param.22) | copy-start | bytes 1572868
  55.7 60.7 %copy-start.36 = (f32[1,2,128,128]{3,2,1,0:T(8,128)S(1)}, f32[1,2,128,128]{3,2,1,0:T(8,128)}, u32[]{:S(2)}) copy-start(f32[1,2,128,128]{3,2,1,0:T(8,128)} %param.26) | copy-start | bytes 393220
  56.2 61.5 %copy-start.54 = (f32[2]{0:T(128)S(1)}, f32[2]{0:T(128)}, u32[]{:S(2)}) copy-start(f32[2]{0:T(128)} %constant.288.clone) | copy-start | bytes 28
  57.2 66.7 %all-to-all-start.3 = ((f32[64,1,512]{2,1,0:T(1,128)}), f32[64,1,512]{2,1,0:T(1,128)S(1)}, u32[]{:S(2)}, u32[]{:S(2)}) async-start(f32[64,1,512]{2,1,0:T(1,128)} %reshape.1326), calls=%async_computation.3 | async-start | bytes 262144 | tf_op jit(solution)/shard_map/all_to_all | solution.py:139
  68.4 49.6 %copy-start.41 = (f32[16,128]{1,0:T(8,128)}, f32[16,128]{1,0:T(8,128)S(1)}, u32[]{:S(2)}) copy-start(f32[16,128]{1,0:T(8,128)S(1)} %multiply_cosine_fusion.3) | copy-start | bytes 24580
  117.1 4.0 copy-start.30
  117.1 4.0 copy-start.32
  117.9 3.3 copy-start.34
  118.0 74.4 %copy-start.1 = (f32[1,2,128,128]{3,2,0,1:T(8,128)}, f32[1,2,128,128]{3,2,0,1:T(8,128)S(1)}, u32[]{:S(2)}) copy-start(f32[1,2,128,128]{3,2,0,1:T(8,128)S(1)} %get-tuple-element.31) | copy-start | bytes 393220
  123.8 23.1 %all-to-all-start.8 = ((f32[64,1,512]{2,1,0:T(1,128)}), f32[64,1,512]{2,1,0:T(1,128)S(1)}, u32[]{:S(2)}, u32[]{:S(2)}) async-start(f32[64,1,512]{2,1,0:T(1,128)} %reshape.1336), calls=%async_computation.8 | async-start | bytes 262144 | tf_op jit(solution)/shard_map/all_to_all | solution.py:139
  146.9 28.4 %all-to-all-start = ((f32[64,1,2048]{2,1,0:T(1,128)}), f32[64,1,2048]{2,1,0:T(1,128)S(1)}, u32[]{:S(2)}, u32[]{:S(2)}) async-start(f32[64,1,2048]{2,1,0:T(1,128)} %reshape.1320), calls=%async_computation | async-start | bytes 1048576 | tf_op jit(solution)/shard_map/all_to_all | solution.py:114
  190.2 3.1 copy-start.25
  192.9 1.5 copy-start.38
  193.0 1.5 copy-start.52
  196.6 9.8 %copy-start.12 = (f32[1,16,2048]{2,1,0:T(8,128)S(1)}, f32[1,16,2048]{2,1,0:T(8,128)}, u32[]{:S(2)}) copy-start(f32[1,16,2048]{2,1,0:T(8,128)} %copy-done.11) | copy-start | bytes 393220
  196.6 10.8 %copy-start.21 = (f32[16,2048]{1,0:T(8,128)S(1)}, f32[16,2048]{1,0:T(8,128)}, u32[]{:S(2)}) copy-start(f32[16,2048]{1,0:T(8,128)} %get-tuple-element.12) | copy-start | bytes 393220
  196.6 10.8 %copy-start.22 = (f32[16,2048]{1,0:T(8,128)S(1)}, f32[16,2048]{1,0:T(8,128)}, u32[]{:S(2)}) copy-start(f32[16,2048]{1,0:T(8,128)} %get-tuple-element.13) | copy-start | bytes 393220
  196.7 10.8 %copy-start.55 = (f32[2]{0:T(128)S(1)}, f32[2]{0:T(128)}, u32[]{:S(2)}) copy-start(f32[2]{0:T(128)} %constant.288.clone) | copy-start | bytes 28
  199.5 23.5 %all-to-all-start.1 = ((f32[64,1,2048]{2,1,0:T(1,128)}), f32[64,1,2048]{2,1,0:T(1,128)S(1)}, u32[]{:S(2)}, u32[]{:S(2)}) async-start(f32[64,1,2048]{2,1,0:T(1,128)} %reshape.1322), calls=%async_computation.1 | async-start | bytes 1048576 | tf_op jit(solution)/shard_map/all_to_all | solution.py:114
  207.5 22.5 %copy-start.13 = (f32[16,2048]{1,0:T(8,128)}, f32[16,2048]{1,0:T(8,128)S(1)}, u32[]{:S(2)}) copy-start(f32[16,2048]{1,0:T(8,128)S(1)} %get-tuple-element.23) | copy-start | bytes 393220
  227.5 1.7 copy-start.49
  230.1 1.8 copy-start.3
  230.1 1.8 copy-start.5
  235.8 14.2 %copy-start.37 = (f32[1,2,128,128]{3,2,1,0:T(8,128)S(1)}, f32[1,2,128,128]{3,2,1,0:T(8,128)}, u32[]{:S(2)}) copy-start(f32[1,2,128,128]{3,2,1,0:T(8,128)} %param.27) | copy-start | bytes 393220
  235.8 15.0 %copy-start.17 = (f32[2,32,1024]{2,1,0:T(8,128)S(1)}, f32[2,32,1024]{2,1,0:T(8,128)}, u32[]{:S(2)}) copy-start(f32[2,32,1024]{2,1,0:T(8,128)} %get-tuple-element.51) | copy-start | bytes 786436
  243.8 23.5 %all-to-all-start.2 = ((f32[64,1,2048]{2,1,0:T(1,128)}), f32[64,1,2048]{2,1,0:T(1,128)S(1)}, u32[]{:S(2)}, u32[]{:S(2)}) async-start(f32[64,1,2048]{2,1,0:T(1,128)} %reshape.1324), calls=%async_computation.2 | async-start | bytes 1048576 | tf_op jit(solution)/shard_map/all_to_all | solution.py:114
  283.7 2.2 copy-start.7
  283.7 2.2 copy-start.9
  318.4 1.7 copy-start.35
  318.4 1.7 copy-start.42
  369.0 1.4 copy-start.47
  369.0 3.2 copy-start.40
  369.0 3.2 copy-start.51
  370.4 2.8 copy-start.19
  370.4 2.8 copy-start.24
  372.8 1.5 copy-start.39
  372.8 1.5 copy-start.53
  376.5 9.5 %copy-start.16 = (f32[2,16,2048]{2,1,0:T(8,128)S(1)}, f32[2,16,2048]{2,1,0:T(8,128)}, u32[]{:S(2)}) copy-start(f32[2,16,2048]{2,1,0:T(8,128)} %get-tuple-element.48) | copy-start | bytes 786436
  379.4 7.8 %copy-start.20 = (f32[16,2048]{1,0:T(8,128)S(1)}, f32[16,2048]{1,0:T(8,128)}, u32[]{:S(2)}) copy-start(f32[16,2048]{1,0:T(8,128)} %get-tuple-element.14) | copy-start | bytes 393220
  379.4 23.7 %all-to-all-start.6 = ((f32[64,1,2048]{2,1,0:T(1,128)}), f32[64,1,2048]{2,1,0:T(1,128)}, u32[]{:S(2)}, u32[]{:S(2)}) async-start(f32[64,1,2048]{2,1,0:T(1,128)} %reshape.1332), calls=%async_computation.6 | async-start | bytes 1048576 | tf_op jit(solution)/shard_map/all_to_all | solution.py:114
  412.9 3.3 copy-start.50
  448.4 14.0 %copy-start.14 = (f32[2,32,1024]{2,1,0:T(8,128)S(1)}, f32[2,32,1024]{2,1,0:T(8,128)}, u32[]{:S(2)}) copy-start(f32[2,32,1024]{2,1,0:T(8,128)} %get-tuple-element.50) | copy-start | bytes 786436
  456.4 23.3 %all-to-all-start.7 = ((f32[64,1,2048]{2,1,0:T(1,128)}), f32[64,1,2048]{2,1,0:T(1,128)S(1)}, u32[]{:S(2)}, u32[]{:S(2)}) async-start(f32[64,1,2048]{2,1,0:T(1,128)} %reshape.1334), calls=%async_computation.7 | async-start | bytes 1048576 | tf_op jit(solution)/shard_map/all_to_all | solution.py:114
  496.7 2.2 copy-start.8
  496.7 2.2 copy-start.10
  504.2 23.3 %all-to-all-start.9 = ((f32[64,1,2048]{2,1,0:T(1,128)}), f32[64,1,2048]{2,1,0:T(1,128)S(1)}, u32[]{:S(2)}, u32[]{:S(2)}) async-start(f32[64,1,2048]{2,1,0:T(1,128)} %reshape.1338), calls=%async_computation.9 | async-start | bytes 1048576 | tf_op jit(solution)/shard_map/all_to_all | solution.py:114
  510.2 137.2 %all-reduce.7.cloned.1.call-start = ((), (), s32[]{:S(2)}) async-start(), calls=%async_computation.10 | async-start | bytes 524288 | tf_op jit(solution)/shard_map/psum | solution.py:123
  (18 other events, 18.8 us)
Sparse Core Ops, SparseCore 0:
  535.5 111.8 all-reduce.6
where the time goes:
time: 667 us; the launch traced here: 656 us
  waiting for transfers between devices  196 us (29%)
  local copies, waits for them, and re-layouts  173 us (26%)
  blocking collectives  138 us (21%)
  starting transfers between devices  63.9 us (10%)
  other arithmetic  52 us (8%)
  between operations  18.9 us (3%)
  matrix products  14.5 us (2%)
    psum x1, waiting for transfers between devices, image_total(): return lax.psum(local_image(fields), 'freq')  111 us
    all_gather x2, blocking collectives, body(): lax.all_gather(velocity[depth_index:depth_index + 1], 'freq', axis=2, til...  91.1 us
    all_to_all x6, waiting for transfers between devices, swap_lines(): lax.all_to_all(fields, 'slab', split_axis=4, concat_axis=3, tiled=True)  84.3 us
    unnamed x141, local copies, waits for them, and re-layouts  83.9 us
    all_to_all x2, blocking collectives, swap_lines(): lax.all_to_all(fields, 'slab', split_axis=4, concat_axis=3, tiled=True)  46.8 us
    all_to_all x6, starting transfers between devices, swap_lines(): lax.all_to_all(fields, 'slab', split_axis=4, concat_axis=3, tiled=True)  42.2 us
    all_to_all x17, local copies, waits for them, and re-layouts, swap_lines(): lax.all_to_all(fields, 'slab', split_axis=4, concat_axis=3, tiled=True)  33.5 us
    another operation x5, local copies, waits for them, and re-layouts  27 us
  transfers between devices with their start and end apart: 9, of which 7 were waited for; matrix products, arithmetic and copies ran while one was open for 6% of the time, Pallas kernels for 0%

commit v1 on v0

v1 whole, which is shorter than its diff:
```python
import functools
import math

import jax
import jax.numpy as jnp
import numpy as np
from jax import lax
from jax.experimental import pallas as pl
from jax.experimental.pallas import tpu as pltpu
from jax.sharding import PartitionSpec as P

F32 = jnp.float32
BF16 = jnp.bfloat16
MESH = pl.DeviceIdType.MESH

NX = 2048
NY = 1024
SLABS = 64
GROUPS = 8
ROWS = 16
spacing = 12.5
depth_step = 10.0


def split_table(table):
    high = table.astype(jnp.bfloat16)
    low = (table - high.astype(np.float64)).astype(jnp.bfloat16)
    return high, low


def angle(product, period):
    turns = 2.0 * math.pi * (product % period) / period
    return np.cos(turns), -np.sin(turns)


@functools.lru_cache(maxsize=None)
def tables():
    sixteen = np.arange(16)
    cos, sin = angle(sixteen[:, None] * sixteen[None, :], 16)
    eye = np.eye(ROWS)
    left_x = np.concatenate([np.kron(cos, eye), np.kron(sin, eye)], 1)
    index = np.arange(256)
    left_y = np.concatenate(angle(index[:, None] * index[None, :], 256), 1)
    lefts = []
    for table in (left_x, left_y):
        high, low = split_table(table)
        lefts.append(np.concatenate([high, high, low], 1))
    inner = np.arange(128)
    cos, sin = angle(inner[:, None] * inner[None, :], 128)
    full = np.zeros((4, 2, 2, 32, 4, 2, 2, 32))
    for field in range(2):
        for c, d, block in ((0, 0, cos), (0, 1, sin), (1, 0, -sin), (1, 1, cos)):
            full[:, c, field, :, :, d, field, :] = block.reshape(4, 32, 4, 32)
    high, low = split_table(full.reshape(512, 512))
    right_x = np.concatenate([high, high, low], 0)
    quarter, outer, column = np.arange(4), np.arange(16), np.arange(32)
    position = quarter[:, None] * 32 + column[None, :]
    product = outer[None, :, None] * position[:, None, :]
    twist_x = []
    for part in angle(product, NX):
        part = np.broadcast_to(part[:, :, None, None, :], (4, 16, 16, 4, 32))
        twist_x.append(part.reshape(1024, 128).astype(np.float32))
    product = np.arange(4)[:, None] * np.arange(256)[None, :]
    twist_y = []
    for part in angle(product, NY):
        part = np.broadcast_to(part.reshape(1024, 1), (1024, 128))
        twist_y.append(part.astype(np.float32))
    return (lefts[0], lefts[1], right_x, *twist_x, *twist_y)


def lanes(rows=1):
    return lax.broadcasted_iota(jnp.int32, (rows, 128), 1)


def turn(x):
    sign = jnp.where(lanes() < 64, -1.0, 1.0)
    return pltpu.roll(x, 64, 1) * sign


def conjugate(x):
    return x * jnp.where(lanes() < 64, 1.0, -1.0)


def halves(x):
    high = x.astype(BF16)
    return high, (x - high.astype(F32)).astype(BF16)


def left_product(table_ref, blocks, direction):
    columns = []
    for x in blocks:
        y = turn(x) * direction if direction != 1 else turn(x)
        high_x, low_x = halves(x)
        high_y, low_y = halves(y)
        columns.append(jnp.concatenate([high_x, high_y, low_x, low_y, high_x, high_y], 0))
    operand = jnp.concatenate(columns, 1)
    total = jnp.dot(table_ref[...], operand, preferred_element_type=F32)
    return [total[:, 128 * k : 128 * (k + 1)] for k in range(len(blocks))]


def right_product(table_ref, blocks):
    highs, lows = zip(*[halves(x) for x in blocks])
    operand = jnp.concatenate([*highs, *lows, *highs], 1)
    total = jnp.dot(operand, table_ref[...], preferred_element_type=F32)
    return [total[:, 128 * k : 128 * (k + 1)] for k in range(4)]


def rotated(x, factor_real, factor_imag):
    return x * factor_real + turn(x) * factor_imag


def at(start, size, unit):
    return pl.ds(pl.multiple_of(start, unit), size)


def outer_x(source, target, left_ref, twist, direction):
    def step(i, carry):
        rows = [at(512 * i + 256 * k, 256, 256) for k in range(2)]
        blocks = [source[r, :] for r in rows]
        if direction < 0:
            blocks = [rotated(b, twist[0][r, :], -twist[1][r, :]) for b, r in zip(blocks, rows)]
        blocks = left_product(left_ref, blocks, direction)
        if direction > 0:
            blocks = [rotated(b, twist[0][r, :], twist[1][r, :]) for b, r in zip(blocks, rows)]
        for b, r in zip(blocks, rows):
            target[r, :] = b
        return carry

    lax.fori_loop(0, 2, step, 0)


def inner_x(source, target, right_ref, before, after):
    def step(i, carry):
        rows = [at(256 * k + 128 * i, 128, 128) for k in range(4)]
        blocks = right_product(right_ref, [before(source[r, :], r) for r in rows])
        for b, r in zip(blocks, rows):
            target[r, :] = after(b, r)
        return carry

    lax.fori_loop(0, 2, step, 0)


def forward_y(source, target, left_ref, twist):
    def butterfly(i, carry):
        rows = [at(256 * k + 32 * i, 32, 32) for k in range(4)]
        x0, x1, x2, x3 = [source[r, :] for r in rows]
        even, odd = x0 + x2, x1 + x3
        minus, spun = x0 - x2, turn(x1 - x3)
        results = [even + odd, minus - spun, even - odd, minus + spun]
        for k, r in enumerate(rows):
            value = results[k]
            if k > 0:
                value = rotated(value, twist[0][r, :], twist[1][r, :])
            target[r, :] = value
        return carry

    lax.fori_loop(0, 8, butterfly, 0)
    middle_y(target, target, left_ref, 1)


def middle_y(source, target, left_ref, direction):
    def step(i, carry):
        rows = [at(512 * i + 256 * k, 256, 256) for k in range(2)]
        blocks = left_product(left_ref, [source[r, :] for r in rows], direction)
        for b, r in zip(blocks, rows):
            target[r, :] = b
        return carry

    lax.fori_loop(0, 2, step, 0)


def inverse_y(source, target, left_ref, twist, finish):
    middle_y(source, source, left_ref, -1)

    def butterfly(i, carry):
        rows = [at(256 * k + 32 * i, 32, 32) for k in range(4)]
        x0, x1, x2, x3 = [source[r, :] for r in rows]
        x1, x2, x3 = [
            rotated(x, twist[0][r, :], -twist[1][r, :]) for x, r in zip((x1, x2, x3), rows[1:])
        ]
        even, odd = x0 + x2, x1 + x3
        minus, spun = x0 - x2, turn(x1 - x3)
        results = [even + odd, minus + spun, even - odd, minus - spun]
        for value, r in zip(results, rows):
            target[r, :] = finish(value, r)
        return carry

    lax.fori_loop(0, 8, butterfly, 0)


def series(square, first):
    value = jnp.full_like(square, (-1.0) ** 8 / math.factorial(16 + first))
    for n in range(7, -1, -1):
        value = value * square + (-1.0) ** n / math.factorial(2 * n + first)
    return value


def wavenumber(index, length):
    signed = jnp.where(index >= length // 2, index - length, index)
    return signed.astype(F32) * (2.0 * math.pi / (length * spacing))


def phase_factors(target_real, target_imag, ratio_square, positions):
    def step(i, carry):
        r = at(64 * i, 64, 64)
        row = lax.broadcasted_iota(jnp.int32, (64, 128), 0) + 64 * i
        column = lanes(64) % 32
        index_x, index_y = positions(row, column)
        wave_x, wave_y = wavenumber(index_x, NX), wavenumber(index_y, NY)
        vertical = ratio_square - wave_x * wave_x - wave_y * wave_y
        square = jnp.abs(vertical) * (depth_step * depth_step)
        size = jnp.sqrt(square)
        travels = vertical >= 0
        scale = 1.0 / (NX * NY)
        target_real[r, :] = jnp.where(travels, series(square, 0), jnp.exp(-size)) * scale
        target_imag[r, :] = jnp.where(travels, size * series(square, 1), 0.0) * scale
        return carry

    lax.fori_loop(0, 16, step, 0)


def split_factors(speed, ref_speed, angular):
    turned = angular * depth_step * (1.0 / speed - 1.0 / ref_speed)
    square = turned * turned
    return series(square, 0), turned * series(square, 1)


def strength_of(speed, ref_speed):
    return 0.5 * (1.0 - ref_speed / speed)


def spread(x, group):
    x = jnp.where(lanes() // 32 == group, x, 0.0)
    x = x + pltpu.roll(x, 64, 1)
    return x + pltpu.roll(x, 32, 1)


def regroup(blocks, index):
    group = lanes() // 32
    result = jnp.zeros_like(blocks[0])
    for g, x in enumerate(blocks):
        shift = 32 * (g - index) % 128
        result = jnp.where(group == g, pltpu.roll(x, shift, 1) if shift else x, result)
    return result


def correct_x(source, padded, mixed, target, strength_ref, right_ref):
    padded[256:1280, :] = source[...]
    padded[0:16, :] = jnp.zeros((16, 128), F32)
    padded[16:256, :] = source[768:1008, :]
    padded[1280:1520, :] = source[16:256, :]
    padded[1520:1536, :] = jnp.zeros((16, 128), F32)
    column = lanes() % 32

    def step(i, carry):
        x = padded[at(256 + 64 * i, 64, 64), :]
        behind = pltpu.roll(padded[at(64 * i, 64, 64), :], 97, 1)
        ahead = pltpu.roll(padded[at(512 + 64 * i, 64, 64), :], 31, 1)
        before = jnp.where(column == 0, behind, pltpu.roll(x, 1, 1))
        after = jnp.where(column == 31, ahead, pltpu.roll(x, 127, 1))
        curvature = before + after - 2.0 * x
        r = at(64 * i, 64, 64)
        mixed[r, :] = x + turn(curvature) * strength_ref[r, :]
        return carry

    lax.fori_loop(0, 16, step, 0)
    inner_x(mixed, target, right_ref, lambda x, r: x, lambda x, r: x + mixed[r, :])


def correct_y(padded, mixed, target, strength_ref, left_ref):
    for i in range(8):
        x = padded[8 + 128 * i : 136 + 128 * i, :]
        before = padded[7 + 128 * i : 135 + 128 * i, :]
        after = padded[9 + 128 * i : 137 + 128 * i, :]
        curvature = before + after - 2.0 * x
        r = slice(128 * i, 128 * i + 128)
        mixed[r, :] = x + turn(curvature) * strength_ref[r, :]

    def step(i, carry):
        rows = [at(256 * i + 128 * k, 128, 128) for k in range(2)]
        blocks = [mixed[r, :] for r in rows]
        added = left_product(left_ref, blocks, 1)
        for x, b, r in zip(blocks, added, rows):
            target[r, :] = x + b
        return carry

    lax.fori_loop(0, 4, step, 0)


def build_blocks(bx_ref, by_ref, right_ref, left_ref):
    for k in range(2):
        high, low = halves(by_ref[0, k])
        for place, value in ((k, high), (2 + k, high), (4 + k, low)):
            left_ref[:, 128 * place : 128 * (place + 1)] = value
    real, imag = bx_ref[0, 0].T, bx_ref[0, 1].T
    zero = jnp.zeros_like(real)
    for c in range(2):
        pair = (real, imag) if c == 0 else (-imag, real)
        for field in range(2):
            blocks = [zero] * 4
            blocks[field], blocks[2 + field] = pair
            for quarter in range(4):
                high, low = halves(regroup(blocks, quarter))
                for q in range(4):
                    base = 128 * q + 64 * c + 32 * field
                    for offset, value in ((0, high), (512, high), (1024, low)):
                        right_ref[offset + base : offset + base + 32, 128 * quarter : 128 * (quarter + 1)] = value[
                            32 * q : 32 * q + 32
                        ]


def kernel(
    refv_ref,
    freq_ref,
    wave_ref,
    vel_ref,
    bx_ref,
    by_ref,
    left_x,
    left_y,
    right_x,
    twist_xr,
    twist_xi,
    twist_yr,
    twist_yi,
    out_ref,
    image_ref,
    sent,
    got,
    work_a,
    work_b,
    padded_x,
    padded_y,
    block_right,
    block_left,
    phase_real,
    phase_imag,
    turn_real,
    turn_imag,
    strength_x,
    strength_y,
    vel_all,
    vel_sent,
    vel_got,
    img_sent,
    img_got,
    part,
    shares,
    summed,
    totals,
    send_sem,
    recv_sem,
    small_send,
    small_recv,
    freq_send,
    freq_recv,
):
    group = lax.axis_index("freq")
    me = lax.axis_index("slab")

    barrier = pltpu.get_barrier_semaphore()

    def greet_slab(i, carry):
        pl.semaphore_signal(barrier, inc=1, device_id=(group, lax.rem(me + i, SLABS)), device_id_type=MESH)
        return carry

    def greet_freq(i, carry):
        pl.semaphore_signal(barrier, inc=1, device_id=(lax.rem(group + i, GROUPS), me), device_id_type=MESH)
        return carry

    lax.fori_loop(1, GROUPS, greet_freq, 0)
    lax.fori_loop(1, SLABS, greet_slab, 0)

    def exchange(source, landing, rows, send, recv):
        own = at(me * rows, rows, rows)

        def step(i, carry):
            other = lax.rem(me + i, SLABS)
            pltpu.make_async_remote_copy(
                src_ref=source.at[at(other * rows, rows, rows), :],
                dst_ref=landing.at[own, :],
                send_sem=send,
                recv_sem=recv,
                device_id=(group, other),
                device_id_type=MESH,
            ).start()
            return carry

        pltpu.make_async_copy(source.at[own, :], landing.at[own, :], recv).start()
        lax.fori_loop(1, SLABS, step, 0)

    def arrived(landing, recv):
        pltpu.make_async_copy(landing, landing, recv).wait()

    def left_here(source, rows, send):
        count = rows * (SLABS - 1)
        pltpu.make_async_copy(source.at[0:count, :], source.at[0:count, :], send).wait()

    def share(piece, landing, send, recv):
        def step(i, carry):
            other = lax.rem(group + i, GROUPS)
            pltpu.make_async_remote_copy(
                src_ref=piece(other),
                dst_ref=landing.at[group],
                send_sem=send,
                recv_sem=recv,
                device_id=(other, me),
                device_id_type=MESH,
            ).start()
            return carry

        pltpu.make_async_copy(piece(group), landing.at[group], recv).start()
        lax.fori_loop(1, GROUPS, step, 0)

    def shared_left(landing, send):
        pltpu.make_async_copy(landing.at[0 : GROUPS - 1], landing.at[0 : GROUPS - 1], send).wait()

    def field_out(k):
        exchange(sent.at[k], got.at[k], ROWS, send_sem.at[k], recv_sem.at[k])

    def field_in(k):
        arrived(got.at[k], recv_sem.at[k])

    def pack(a, carry):
        window = at(a * 128, 128, 128)
        blocks = [wave_ref[0, g % 2, g // 2, :, window] for g in range(4)]
        for q in range(4):
            work_a[at(q * 256 + a * 16, 16, 16), :] = regroup(blocks, q)
        return carry

    lax.fori_loop(0, 16, pack, 0)
    twist_x = (twist_xr, twist_xi)
    twist_y = (twist_yr, twist_yi)
    outer_x(work_a, work_b, left_x, twist_x, 1)
    inner_x(work_b, sent.at[0], right_x, lambda x, r: x, lambda x, r: x)

    pl.semaphore_wait(barrier, SLABS - 1 + GROUPS - 1)
    field_out(0)
    share(lambda g: vel_ref, vel_all, freq_send.at[0], freq_recv.at[0])

    angular = jnp.full((1, 128), freq_ref[0], F32) * (2.0 * math.pi)
    speeds = [jnp.full((1, 128), refv_ref[d], F32) for d in range(2)]
    squares = [(angular / v) * (angular / v) for v in speeds]

    def positions_y(row, column):
        index_x = lax.rem(me, 16) + 16 * (lax.div(me, 16) * 32 + column)
        return index_x, row // 256 + 4 * (row % 256)

    phase_factors(phase_real.at[0], phase_imag.at[0], squares[0], positions_y)
    build_blocks(bx_ref, by_ref, block_right, block_left)

    arrived(vel_all, freq_recv.at[0])

    def pack_speed(a, carry):
        f = lax.div(a, 2)
        window = at(lax.rem(a, 2) * 128, 128, 128)
        for d in range(2):
            x = vel_all[f, d, :, window]
            for q in range(4):
                r = at(q * 256 + a * 16, 16, 16)
                speed = spread(x, q)
                strength_x[d, r, :] = strength_of(speed, speeds[d])
                if d == 0:
                    real, imag = split_factors(speed, speeds[d], angular)
                    turn_real[0, r, :] = real
                    turn_imag[0, r, :] = imag
        blocks = [vel_all[f, g % 2, 8 * (g // 2) : 8 * (g // 2) + 8, window] for g in range(4)]
        for q in range(4):
            vel_sent[at((q * 16 + a) * 8, 8, 8), :] = regroup(blocks, q)
        return carry

    lax.fori_loop(0, 16, pack_speed, 0)
    exchange(vel_sent, vel_got, 8, small_send.at[0], small_recv.at[0])

    field_in(0)
    forward_y(got.at[0], work_a, left_y, twist_y)

    def shift(source, target, k):
        def step(i, carry):
            r = at(64 * i, 64, 64)
            target[r, :] = rotated(source[r, :], phase_real[k, r, :], phase_imag[k, r, :])
            return carry

        lax.fori_loop(0, 16, step, 0)

    shift(work_a, work_b, 0)
    inverse_y(work_b, sent.at[1], left_y, twist_y, lambda x, r: x)
    field_out(1)

    arrived(vel_got, small_recv.at[0])

    def unpack_speed(s, carry):
        x = vel_got[at(8 * s, 8, 8), :]
        for d in range(2):
            for h in range(2):
                r = at(16 * s + 8 * h, 8, 8)
                speed = spread(x, 2 * h + d)
                strength_y[d, r, :] = strength_of(speed, speeds[d])
                if d == 1:
                    real, imag = split_factors(speed, speeds[d], angular)
                    turn_real[1, r, :] = real
                    turn_imag[1, r, :] = imag
        return carry

    lax.fori_loop(0, 64, unpack_speed, 0)

    def positions_x(row, column):
        line = me * 16 + row % 16
        index_x = row // 16 % 16 + 16 * (row // 256 * 32 + column)
        return index_x, line // 256 + 4 * (line % 256)

    phase_factors(phase_real.at[1], phase_imag.at[1], squares[1], positions_x)

    field_in(1)
    inner_x(got.at[1], work_a, right_x, lambda x, r: conjugate(x), lambda x, r: conjugate(x))
    outer_x(work_a, work_b, left_x, twist_x, -1)

    def split_x(i, carry):
        r = at(64 * i, 64, 64)
        work_a[r, :] = rotated(work_b[r, :], turn_real[0, r, :], turn_imag[0, r, :])
        return carry

    lax.fori_loop(0, 16, split_x, 0)
    correct_x(work_a, padded_x, work_b, sent.at[2], strength_x.at[0], block_right)
    field_out(2)

    zeros = jnp.zeros((8, 128), F32)
    padded_y[0:8, :] = zeros
    padded_y[1032:1040, :] = zeros
    field_in(2)
    padded_y[8:1032, :] = got[2]
    correct_y(padded_y, work_a, work_b, strength_y.at[0], block_left)

    forward_y(work_b, sent.at[3], left_y, twist_y)
    field_out(3)

    def image_y(s, carry):
        group_of = lanes() // 32
        pieces = []
        for h in range(2):
            x = work_b[at(16 * s + 8 * h, 8, 8), :]
            product = x * pltpu.roll(x, 96, 1)
            pieces.append(product - pltpu.roll(product, 64, 1))
        packed = jnp.where(group_of == 1, pltpu.roll(pieces[1], 32, 1), 0.0)
        img_sent[at(8 * s, 8, 8), :] = jnp.where(group_of == 0, pieces[0], packed)
        return carry

    lax.fori_loop(0, 64, image_y, 0)
    exchange(img_sent, img_got, 8, small_send.at[1], small_recv.at[1])

    field_in(3)
    outer_x(got.at[3], work_a, left_x, twist_x, 1)

    def shifted(x, r):
        return conjugate(rotated(x, phase_real[1, r, :], phase_imag[1, r, :]))

    inner_x(work_a, work_b, right_x, lambda x, r: x, shifted)
    inner_x(work_b, work_a, right_x, lambda x, r: x, lambda x, r: conjugate(x))
    outer_x(work_a, sent.at[4], left_x, twist_x, -1)
    field_out(4)

    def reduce_out(d):
        share(lambda g: part.at[d, at(2 * g, 2, 2)], shares.at[d], freq_send.at[1 + d], freq_recv.at[1 + d])

    def gather_out(d):
        arrived(shares.at[d], freq_recv.at[1 + d])
        total = shares[d, 0]
        for g in range(1, GROUPS):
            total = total + shares[d, g]
        summed[d] = total
        share(lambda g: summed.at[d], totals.at[d], freq_send.at[3 + d], freq_recv.at[3 + d])

    arrived(img_got, small_recv.at[1])

    def image_x(a, carry):
        group_of = lanes() // 32
        for h in range(2):
            result = jnp.zeros((8, 128), F32)
            for q in range(4):
                x = img_got[at((q * 16 + a) * 8, 8, 8), :]
                amount = 32 * (q - h) % 128
                result = jnp.where(group_of == q, pltpu.roll(x, amount, 1) if amount else x, result)
            part[0, a, 8 * h : 8 * h + 8, :] = result
        return carry

    lax.fori_loop(0, 16, image_x, 0)
    reduce_out(0)

    field_in(4)

    def split_y(x, r):
        return rotated(x, turn_real[1, r, :], turn_imag[1, r, :])

    def copy_in(i, carry):
        r = at(64 * i, 64, 64)
        work_b[r, :] = got[4, r, :]
        return carry

    lax.fori_loop(0, 16, copy_in, 0)
    inverse_y(work_b, work_a, left_y, twist_y, split_y)
    padded_y[8:1032, :] = work_a[...]
    correct_y(padded_y, work_b, sent.at[5], strength_y.at[1], block_left)
    field_out(5)
    gather_out(0)

    field_in(5)
    correct_x(got.at[5], padded_x, work_b, work_a, strength_x.at[1], block_right)

    def image_last(a, carry):
        blocks = [work_a[at(q * 256 + a * 16, 16, 16), :] for q in range(4)]
        whole = [regroup(blocks, g) for g in range(4)]
        part[1, a] = whole[0] * whole[1] - whole[2] * whole[3]
        window = at(a * 128, 128, 128)
        for g in range(4):
            out_ref[0, g % 2, g // 2, :, window] = whole[g]
        return carry

    lax.fori_loop(0, 16, image_last, 0)
    reduce_out(1)
    gather_out(1)

    for d in range(2):
        arrived(totals.at[d], freq_recv.at[3 + d])
        for a in range(16):
            image_ref[d, :, 128 * a : 128 * (a + 1)] = totals[d, a // 2, a % 2]

    for k in range(6):
        left_here(sent.at[k], ROWS, send_sem.at[k])
    left_here(vel_sent, 8, small_send.at[0])
    left_here(img_sent, 8, small_send.at[1])
    shared_left(vel_all, freq_send.at[0])
    for d in range(2):
        shared_left(shares.at[d], freq_send.at[1 + d])
        shared_left(totals.at[d], freq_send.at[3 + d])


def body(wavefield, velocity, reference_velocity, frequencies, block_x, block_y):
    state = (1024, 128)
    vmem, smem = pl.BlockSpec(memory_space=pltpu.VMEM), pl.BlockSpec(memory_space=pltpu.SMEM)
    constants = [jnp.asarray(t) for t in tables()]
    call = pl.pallas_call(
        kernel,
        out_shape=(
            jax.ShapeDtypeStruct(wavefield.shape, F32),
            jax.ShapeDtypeStruct((2, ROWS, NX), F32),
        ),
        in_specs=[smem, smem] + [vmem] * (4 + len(constants)),
        out_specs=(vmem, vmem),
        scratch_shapes=[
            pltpu.VMEM((6, *state), F32),
            pltpu.VMEM((6, *state), F32),
            pltpu.VMEM(state, F32),
            pltpu.VMEM(state, F32),
            pltpu.VMEM((1536, 128), F32),
            pltpu.VMEM((1040, 128), F32),
            pltpu.VMEM((1536, 512), BF16),
            pltpu.VMEM((128, 768), BF16),
            pltpu.VMEM((2, *state), F32),
            pltpu.VMEM((2, *state), F32),
            pltpu.VMEM((2, *state), F32),
            pltpu.VMEM((2, *state), F32),
            pltpu.VMEM((2, *state), F32),
            pltpu.VMEM((2, *state), F32),
            pltpu.VMEM((GROUPS, 2, ROWS, 256), F32),
            pltpu.VMEM((512, 128), F32),
            pltpu.VMEM((512, 128), F32),
            pltpu.VMEM((512, 128), F32),
            pltpu.VMEM((512, 128), F32),
            pltpu.VMEM((2, 16, ROWS, 128), F32),
            pltpu.VMEM((2, GROUPS, 2, ROWS, 128), F32),
            pltpu.VMEM((2, 2, ROWS, 128), F32),
            pltpu.VMEM((2, GROUPS, 2, ROWS, 128), F32),
            pltpu.SemaphoreType.DMA((6,)),
            pltpu.SemaphoreType.DMA((6,)),
            pltpu.SemaphoreType.DMA((2,)),
            pltpu.SemaphoreType.DMA((2,)),
            pltpu.SemaphoreType.DMA((5,)),
            pltpu.SemaphoreType.DMA((5,)),
        ],
        compiler_params=pltpu.CompilerParams(
            collective_id=0, has_side_effects=True, vmem_limit_bytes=48 * 1024 * 1024
        ),
    )
    return call(reference_velocity, frequencies, wavefield, velocity, block_x, block_y, *constants)


def solution(mesh):
    in_specs = (
        P("freq", None, None, "slab", None),
        P(None, "slab", "freq"),
        P(),
        P("freq"),
        P("freq", None, None, None),
        P("freq", None, None, None),
    )
    out_specs = (P("freq", None, None, "slab", None), P(None, "slab", None))
    return jax.shard_map(body, mesh=mesh, in_specs=in_specs, out_specs=out_specs, check_vma=False)
```

time: 667 us -> 181 us (0.27)
  the two profiles are of different devices: /device:TPU:8 before, /device:TPU:1 now
where the time goes in v1:
time: 181 us
  Pallas kernels  167 us (92%)
  local copies, waits for them, and re-layouts  12.2 us (7%)
    pallas_call x1, Pallas kernels, body(): call(reference_velocity, frequencies, wavefield, velocity, block_x, block...  167 us
    unnamed x24, local copies, waits for them, and re-layouts  12.2 us

profile of v1, /device:TPU:1, one launch (start us, length us, event | category | flops | bytes accessed | tf_op | source)
XLA Modules:
  0.0 180.8 jit_solution(1793796044772155121)
XLA Ops:
  1.3 0.0 copy-start
  1.3 1.1 copy-done
  2.4 0.0 copy-start.1
  2.4 1.1 copy-done.1
  3.5 0.0 copy-start.2
  3.5 1.0 copy-done.2
  4.6 0.0 copy-start.3
  4.6 1.0 copy-done.3
  5.6 0.0 copy-start.4
  5.6 1.0 copy-done.4
  6.7 0.0 copy-start.5
  6.7 1.0 copy-done.5
  7.7 0.0 copy-start.6
  7.7 1.0 copy-done.6
  8.8 0.0 copy-start.7
  8.8 0.9 copy-done.7
  9.7 0.0 copy-start.8
  9.7 0.9 copy-done.8
  10.6 0.0 copy-start.9
  10.6 0.8 copy-done.9
  11.3 0.0 copy-start.10
  11.3 0.7 copy-done.10
  12.0 167.3 %shard_map.140 = (f32[1,2,2,16,2048]{4,3,2,1,0:T(8,128)S(1)}, f32[2,16,2048]{2,1,0:T(8,128)S(1)}) custom-call(f32[2]{0:T(128)S(1)} %copy-done.10, f32[1]{0:T(128)S(6)} %copy.17.freq_ref, f32[1,2,2,16,2048]{4,3,2,1,0:T(8,128)S(1)} %copy-done.2, f32[2,16,256]{2,1,0:T(8,128)S(1)} %copy-done.9, f32[1,2,128,128]{3,2,1,0:T(8,128)S(1)} %copy-done.7, ...), custom_call_target="tpu_custom_call" | custom-call | tf_op jit(solution)/shard_map/pallas_call | solution.py:684
  179.3 0.8 copy.18
  180.1 0.7 copy.19
Async XLA Ops:
  1.3 1.1 copy-start
  2.4 1.1 copy-start.1
  3.5 1.0 copy-start.2
  4.6 1.0 copy-start.3
  5.6 1.0 copy-start.4
  6.7 1.0 copy-start.5
  7.7 1.0 copy-start.6
  8.8 0.9 copy-start.7
  9.7 0.9 copy-start.8
  10.6 0.8 copy-start.9
  11.3 0.7 copy-start.10

commit v2 on v1

v2 whole, which is shorter than its diff:
```python
import functools
import math

import jax
import jax.numpy as jnp
import numpy as np
from jax import lax
from jax.experimental import pallas as pl
from jax.experimental.pallas import tpu as pltpu
from jax.sharding import PartitionSpec as P

F32 = jnp.float32
BF16 = jnp.bfloat16
MESH = pl.DeviceIdType.MESH

NX = 2048
NY = 1024
SLABS = 64
GROUPS = 8
HALF = 8
STRIDE = 27
spacing = 12.5
depth_step = 10.0


def split_table(table):
    high = table.astype(jnp.bfloat16)
    low = (table - high.astype(np.float64)).astype(jnp.bfloat16)
    return high, low


def angle(product, period):
    turns = 2.0 * math.pi * (product % period) / period
    return np.cos(turns), -np.sin(turns)


@functools.lru_cache(maxsize=None)
def tables():
    sixteen = np.arange(16)
    cos, sin = angle(sixteen[:, None] * sixteen[None, :], 16)
    eye = np.eye(HALF)
    high, low = split_table(np.concatenate([np.kron(cos, eye), np.kron(sin, eye)], 1))
    left_x = np.concatenate([high, high, low], 1)
    place = np.arange(16)[:, None] * 16 + np.arange(8)[None, :]
    places = [(place + 8 * h).reshape(128) for h in range(2)]
    order = np.concatenate(places)
    left_y = []
    for h in range(2):
        high, low = split_table(np.concatenate(angle(order[:, None] * places[h][None, :], 256), 1))
        left_y.append(np.concatenate([high, high, low], 1))
    left_y = np.stack(left_y)
    inner = np.arange(128)
    cos, sin = angle(inner[:, None] * inner[None, :], 128)
    full = np.zeros((4, 2, 2, 32, 4, 2, 2, 32))
    for field in range(2):
        for c, d, block in ((0, 0, cos), (0, 1, sin), (1, 0, -sin), (1, 1, cos)):
            full[:, c, field, :, :, d, field, :] = block.reshape(4, 32, 4, 32)
    right_x = np.concatenate(split_table(full.reshape(512, 512)), 0)
    quarter, outer, column = np.arange(4), np.arange(16), np.arange(32)
    position = quarter[:, None] * 32 + column[None, :]
    product = outer[None, :, None] * position[:, None, :]
    twist_x = []
    for part in angle(product, NX):
        part = np.broadcast_to(part[:, :, None, None, :], (4, 16, HALF, 4, 32))
        twist_x.append(part.reshape(512, 128))
    product = np.arange(4)[None, :, None] * np.stack(places)[:, None, :]
    twist_y = []
    for part in angle(product, NY):
        part = np.broadcast_to(part.reshape(2, 512, 1), (2, 512, 128))
        twist_y.append(part)
    return left_x, np.stack(twist_x).astype(np.float32), right_x, left_y, np.stack(twist_y).astype(np.float32)


def lanes(rows=1):
    return lax.broadcasted_iota(jnp.int32, (rows, 128), 1)


def turn(x):
    sign = jnp.where(lanes() < 64, -1.0, 1.0)
    return pltpu.roll(x, 64, 1) * sign


def unturn(x):
    sign = jnp.where(lanes() < 64, 1.0, -1.0)
    return pltpu.roll(x, 64, 1) * sign


def conjugate(x):
    return x * jnp.where(lanes() < 64, 1.0, -1.0)


def halves(x):
    high = x.astype(BF16)
    return high, (x - high.astype(F32)).astype(BF16)


def left_operand(blocks, direction):
    columns = []
    for x in blocks:
        y = turn(x) if direction > 0 else unturn(x)
        high_x, low_x = halves(x)
        high_y, low_y = halves(y)
        columns.append(jnp.concatenate([high_x, high_y, low_x, low_y, high_x, high_y], 0))
    return jnp.concatenate(columns, 1)


def product(left, right):
    return jnp.dot(left, right, preferred_element_type=F32)


def in_blocks(total):
    return [total[:, 128 * k : 128 * (k + 1)] for k in range(total.shape[1] // 128)]


def right_product(table_ref, blocks):
    highs, lows = zip(*[halves(x) for x in blocks])
    return in_blocks(product(jnp.concatenate([*highs, *highs, *lows], 1), table_ref[...]))


def rotated(x, factor_real, factor_imag):
    return x * factor_real + turn(x) * factor_imag


def rotated_back(x, factor_real, factor_imag):
    return x * factor_real + unturn(x) * factor_imag


def at(start, size, unit):
    return pl.ds(pl.multiple_of(start, unit), size)


def quarters(ref):
    return [ref[128 * k : 128 * (k + 1), :] for k in range(4)]


def put(ref, blocks):
    for k, x in enumerate(blocks):
        ref[128 * k : 128 * (k + 1), :] = x


def outer_x(blocks, left_ref, twist, direction):
    rows = [slice(128 * k, 128 * (k + 1)) for k in range(4)]
    if direction < 0:
        blocks = [rotated_back(b, twist[0, r, :], twist[1, r, :]) for b, r in zip(blocks, rows)]
    blocks = in_blocks(product(left_ref[...], left_operand(blocks, direction)))
    if direction > 0:
        blocks = [rotated(b, twist[0, r, :], twist[1, r, :]) for b, r in zip(blocks, rows)]
    return blocks


def inverse_inner_x(blocks, right_ref):
    return [conjugate(b) for b in right_product(right_ref, [conjugate(b) for b in blocks])]


def butterfly_forward(source, target, twist, h):
    def step(i, carry):
        rows = [at(128 * k + 32 * i, 32, 32) for k in range(4)]
        x0, x1, x2, x3 = [source[r, :] for r in rows]
        even, odd = x0 + x2, x1 + x3
        minus, spun = x0 - x2, turn(x1 - x3)
        results = [even + odd, minus - spun, even - odd, minus + spun]
        for k, r in enumerate(rows):
            value = results[k]
            if k > 0:
                value = rotated(value, twist[0, h, r, :], twist[1, h, r, :])
            target[r, :] = value
        return carry

    lax.fori_loop(0, 4, step, 0)


def butterfly_inverse(source, target, twist, h, finish):
    def step(i, carry):
        rows = [at(128 * k + 32 * i, 32, 32) for k in range(4)]
        x0, x1, x2, x3 = [source[r, :] for r in rows]
        x1, x2, x3 = [
            rotated_back(x, twist[0, h, r, :], twist[1, h, r, :])
            for x, r in zip((x1, x2, x3), rows[1:])
        ]
        even, odd = x0 + x2, x1 + x3
        minus, spun = x0 - x2, turn(x1 - x3)
        results = [even + odd, minus + spun, even - odd, minus - spun]
        for value, r in zip(results, rows):
            target[r, :] = finish(value, r)
        return carry

    lax.fori_loop(0, 4, step, 0)


def series(square, first):
    value = jnp.full_like(square, 1.0 / math.factorial(16 + first))
    for n in range(7, -1, -1):
        value = value * square + (-1.0) ** n / math.factorial(2 * n + first)
    return value


def wavenumber(index, length):
    signed = jnp.where(index >= length // 2, index - length, index)
    return signed.astype(F32) * (2.0 * math.pi / (length * spacing))


def phase_factors(target_real, target_imag, ratio_square, positions):
    def step(i, carry):
        r = at(64 * lax.rem(i, 8), 64, 64)
        h = lax.div(i, 8)
        row = lax.broadcasted_iota(jnp.int32, (64, 128), 0) + 64 * lax.rem(i, 8)
        column = lanes(64) % 32
        index_x, index_y = positions(h, row, column)
        wave_x, wave_y = wavenumber(index_x, NX), wavenumber(index_y, NY)
        vertical = ratio_square - wave_x * wave_x - wave_y * wave_y
        square = jnp.abs(vertical) * (depth_step * depth_step)
        size = jnp.sqrt(square)
        travels = vertical >= 0
        scale = 1.0 / (NX * NY)
        target_real[h, r, :] = jnp.where(travels, series(square, 0), jnp.exp(-size)) * scale
        target_imag[h, r, :] = jnp.where(travels, size * series(square, 1), 0.0) * scale
        return carry

    lax.fori_loop(0, 16, step, 0)


def split_factors(speed, ref_speed, angular):
    turned = angular * depth_step * (1.0 / speed - 1.0 / ref_speed)
    square = turned * turned
    return series(square, 0), turned * series(square, 1)


def strength_of(speed, ref_speed):
    return 0.5 * (1.0 - ref_speed / speed)


def spread(x, group):
    x = jnp.where(lanes() // 32 == group, x, 0.0)
    x = x + pltpu.roll(x, 64, 1)
    return x + pltpu.roll(x, 32, 1)


def regroup(blocks, index):
    group = lanes() // 32
    result = jnp.zeros_like(blocks[0])
    for g, x in enumerate(blocks):
        shift = 32 * (g - index) % 128
        result = jnp.where(group == g, pltpu.roll(x, shift, 1) if shift else x, result)
    return result


def correct_x(blocks, padded, strength, right_ref):
    for k in range(4):
        padded[128 * (k + 1) : 128 * (k + 2), :] = blocks[k]
    padded[0:8, :] = jnp.zeros((8, 128), F32)
    padded[8:128, :] = blocks[3][0:120]
    padded[640:760, :] = blocks[0][8:128]
    padded[760:768, :] = jnp.zeros((8, 128), F32)
    column = lanes() % 32
    mixed = []
    for k in range(4):
        x = padded[128 * (k + 1) : 128 * (k + 2), :]
        behind = pltpu.roll(padded[128 * k : 128 * (k + 1), :], 97, 1)
        ahead = pltpu.roll(padded[128 * (k + 2) : 128 * (k + 3), :], 31, 1)
        before = jnp.where(column == 0, behind, pltpu.roll(x, 1, 1))
        after = jnp.where(column == 31, ahead, pltpu.roll(x, 127, 1))
        curvature = before + after - 2.0 * x
        mixed.append(x + turn(curvature) * strength[128 * k : 128 * (k + 1), :])
    return [x + b for x, b in zip(mixed, right_product(right_ref, mixed))]


def correct_y(padded, mixed, target, strength, left_ref):
    line = lax.broadcasted_iota(jnp.int32, (128, 128), 0) % 8
    for i in range(4):
        for h in range(2):

            def near(half, offset):
                return padded[half, 8 + offset + 128 * i : 136 + offset + 128 * i, :]

            x = near(h, 0)
            before = jnp.where(line == 0, near(1 - h, 7 if h else -1), near(h, -1))
            after = jnp.where(line == 7, near(1 - h, 1 if h else -7), near(h, 1))
            curvature = before + after - 2.0 * x
            r = slice(128 * i, 128 * i + 128)
            mixed[h, r, :] = x + turn(curvature) * strength[h, r, :]

    def step(i, carry):
        rows = [at(256 * i + 64 * k, 64, 64) for k in range(4)]
        blocks = [jnp.concatenate([mixed[0, r, :], mixed[1, r, :]], 0) for r in rows]
        added = in_blocks(product(left_ref[...], left_operand(blocks, 1)))
        for x, b, r in zip(blocks, added, rows):
            value = x + b
            target[0, r, :] = value[0:64]
            target[1, r, :] = value[64:128]
        return carry

    lax.fori_loop(0, 2, step, 0)


def by_halves(matrix):
    low = [matrix[16 * s : 16 * s + 8] for s in range(8)]
    high = [matrix[16 * s + 8 : 16 * s + 16] for s in range(8)]
    return jnp.concatenate(low + high, 0)


def build_blocks(bx_ref, by_ref, right_ref, left_ref):
    for k in range(2):
        high, low = halves(by_halves(by_halves(by_ref[0, k]).T).T)
        for place, value in ((k, high), (2 + k, high), (4 + k, low)):
            left_ref[:, 128 * place : 128 * (place + 1)] = value
    real, imag = bx_ref[0, 0].T, bx_ref[0, 1].T
    zero = jnp.zeros_like(real)
    for c in range(2):
        pair = (real, imag) if c == 0 else (-imag, real)
        for field in range(2):
            blocks = [zero] * 4
            blocks[field], blocks[2 + field] = pair
            for quarter in range(4):
                high, low = halves(regroup(blocks, quarter))
                columns = slice(128 * quarter, 128 * (quarter + 1))
                for q in range(4):
                    base = 128 * q + 64 * c + 32 * field
                    for offset, value in ((0, high), (512, low), (1024, high)):
                        right_ref[offset + base : offset + base + 32, columns] = value[32 * q : 32 * q + 32]


def kernel(
    refv_ref,
    freq_ref,
    wave_hbm,
    vel_hbm,
    bx_hbm,
    by_hbm,
    left_x_hbm,
    twist_x_hbm,
    right_x_hbm,
    left_y_hbm,
    twist_y_hbm,
    out_ref,
    image_ref,
    wave_ref,
    vel_ref,
    bx_ref,
    by_ref,
    left_x,
    twist_x,
    right_x,
    left_y,
    twist_y,
    sent,
    got,
    work_a,
    work_b,
    operands,
    padded_x,
    padded_y,
    block_right,
    block_left,
    phase_real,
    phase_imag,
    turn_real,
    turn_imag,
    strength_x,
    strength_y,
    vel_all,
    vel_sent,
    vel_got,
    img_sent,
    img_got,
    part,
    shares,
    summed,
    totals,
    send_sem,
    recv_sem,
    small_send,
    small_recv,
    freq_send,
    freq_recv,
    load_sem,
):
    group = lax.axis_index("freq")
    me = lax.axis_index("slab")

    loads = []
    pairs = (
        (wave_hbm, wave_ref),
        (left_x_hbm, left_x),
        (twist_x_hbm, twist_x),
        (right_x_hbm, right_x.at[0:1024, :]),
        (vel_hbm, vel_ref),
        (left_y_hbm, left_y),
        (twist_y_hbm, twist_y),
        (bx_hbm, bx_ref),
        (by_hbm, by_ref),
    )
    for k, (source, target) in enumerate(pairs):
        loads.append(pltpu.make_async_copy(source, target, load_sem.at[k]))
        loads[-1].start()

    barrier = pltpu.get_barrier_semaphore()

    def greet_slab(i, carry):
        pl.semaphore_signal(barrier, inc=1, device_id=(group, lax.rem(me + i, SLABS)), device_id_type=MESH)
        return carry

    def greet_freq(i, carry):
        pl.semaphore_signal(barrier, inc=1, device_id=(lax.rem(group + i, GROUPS), me), device_id_type=MESH)
        return carry

    lax.fori_loop(1, GROUPS, greet_freq, 0)
    lax.fori_loop(1, SLABS, greet_slab, 0)

    def exchange(source, landing, send, recv):
        own = at(me * HALF, HALF, HALF)

        def step(i, carry):
            other = lax.rem(me + i * STRIDE, SLABS)
            pltpu.make_async_remote_copy(
                src_ref=source.at[at(other * HALF, HALF, HALF), :],
                dst_ref=landing.at[own, :],
                send_sem=send,
                recv_sem=recv,
                device_id=(group, other),
                device_id_type=MESH,
            ).start()
            return carry

        lax.fori_loop(1, SLABS, step, 0)
        pltpu.make_async_copy(source.at[own, :], landing.at[own, :], recv).start()

    def arrived(landing, recv):
        pltpu.make_async_copy(landing, landing, recv).wait()

    def left_here(source, send):
        count = HALF * (SLABS - 1)
        pltpu.make_async_copy(source.at[0:count, :], source.at[0:count, :], send).wait()

    def share(piece, landing, send, recv):
        def step(i, carry):
            other = lax.rem(group + i, GROUPS)
            pltpu.make_async_remote_copy(
                src_ref=piece(other),
                dst_ref=landing.at[group],
                send_sem=send,
                recv_sem=recv,
                device_id=(other, me),
                device_id_type=MESH,
            ).start()
            return carry

        lax.fori_loop(1, GROUPS, step, 0)
        pltpu.make_async_copy(piece(group), landing.at[group], recv).start()

    def shared_left(landing, send):
        pltpu.make_async_copy(landing.at[0 : GROUPS - 1], landing.at[0 : GROUPS - 1], send).wait()

    def field_out(k, h):
        exchange(sent.at[k, h], got.at[k, h], send_sem.at[k, h], recv_sem.at[k, h])

    def field_in(k, h):
        arrived(got.at[k, h], recv_sem.at[k, h])

    def both(step):
        def run(h, carry):
            step(h)
            return carry

        lax.fori_loop(0, 2, run, 0)

    loads[0].wait()
    loads[1].wait()
    loads[2].wait()

    def start_x(h):
        lines = at(8 * h, 8, 8)
        natural = []
        for g in range(4):
            pieces = [wave_ref[0, g % 2, g // 2, lines, 128 * a : 128 * (a + 1)] for a in range(16)]
            natural.append(jnp.concatenate(pieces, 0))
        put(work_a.at[h], outer_x([regroup(natural, q) for q in range(4)], left_x, twist_x, 1))

    both(start_x)
    loads[3].wait()
    loads[4].wait()

    def repeat_table(i, carry):
        right_x[at(1024 + 128 * i, 128, 128), :] = right_x[at(128 * i, 128, 128), :]
        return carry

    lax.fori_loop(0, 4, repeat_table, 0)
    pl.semaphore_wait(barrier, SLABS - 1 + GROUPS - 1)

    def send_x(h):
        put(sent.at[0, h], right_product(right_x, quarters(work_a.at[h])))
        field_out(0, h)

    both(send_x)
    share(lambda g: vel_ref, vel_all, freq_send.at[0], freq_recv.at[0])

    angular = jnp.full((1, 128), freq_ref[0], F32) * (2.0 * math.pi)
    speeds = [jnp.full((1, 128), refv_ref[d], F32) for d in range(2)]
    squares = [(angular / v) * (angular / v) for v in speeds]

    def positions_y(h, row, column):
        index_x = lax.rem(me, 16) + 16 * (lax.div(me, 16) * 32 + column)
        rest = row % 128
        return index_x, row // 128 + 4 * (16 * (rest // 8) + 8 * h + rest % 8)

    phase_factors(phase_real.at[0], phase_imag.at[0], squares[0], positions_y)
    loads[5].wait()
    loads[6].wait()

    def part_in(k, h, source, direction):
        operand = left_operand(quarters(source), direction)
        return in_blocks(product(left_y[h], operand))

    def accumulate(parts, h):
        for k, x in enumerate(parts):
            for m in range(2):
                r = slice(128 * k, 128 * (k + 1))
                value = x[128 * m : 128 * (m + 1)]
                work_b[m, r, :] = value if h == 0 else work_b[m, r, :] + value

    def products_y(h):
        rows = at(128 * h, 128, 128)
        total = product(left_y[0, rows, :], operands[0]) + product(left_y[1, rows, :], operands[1])
        return in_blocks(total)

    for h in range(2):
        field_in(0, h)
        butterfly_forward(got.at[0, h], work_a.at[h], twist_y, h)
        accumulate(part_in(0, h, work_a.at[h], 1), h)

    def shift_y(m):
        blocks = [
            rotated(b, phase_real[0, m, 128 * k : 128 * (k + 1), :], phase_imag[0, m, 128 * k : 128 * (k + 1), :])
            for k, b in enumerate(quarters(work_b.at[m]))
        ]
        operands[m] = left_operand(blocks, -1)

    both(shift_y)

    def back_y(h):
        put(work_a.at[h], products_y(h))
        butterfly_inverse(work_a.at[h], sent.at[1, h], twist_y, h, lambda x, r: x)
        field_out(1, h)

    both(back_y)

    arrived(vel_all, freq_recv.at[0])

    def pack_speed(f, carry):
        for low in range(2):
            a = 2 * f + low
            window = slice(128 * low, 128 * (low + 1))
            for d in range(2):
                x = vel_all[f, d, :, window]
                for q in range(4):
                    r = at(q * 128 + a * 8, 8, 8)
                    speed = spread(x, q)
                    strength = strength_of(speed, speeds[d])
                    for h in range(2):
                        strength_x[d, h, r, :] = strength[8 * h : 8 * h + 8]
                    if d == 0:
                        real, imag = split_factors(speed, speeds[d], angular)
                        for h in range(2):
                            turn_real[0, h, r, :] = real[8 * h : 8 * h + 8]
                            turn_imag[0, h, r, :] = imag[8 * h : 8 * h + 8]
            blocks = [vel_all[f, g % 2, 8 * (g // 2) : 8 * (g // 2) + 8, window] for g in range(4)]
            for q in range(4):
                vel_sent[at((q * 16 + a) * 8, 8, 8), :] = regroup(blocks, q)
        return carry

    lax.fori_loop(0, GROUPS, pack_speed, 0)
    exchange(vel_sent, vel_got, small_send.at[0], small_recv.at[0])
    loads[7].wait()
    loads[8].wait()
    build_blocks(bx_ref, by_ref, block_right, block_left)

    def correct_lines(h):
        field_in(1, h)
        blocks = inverse_inner_x(quarters(got.at[1, h]), right_x)
        blocks = outer_x(blocks, left_x, twist_x, -1)
        blocks = [
            rotated(b, turn_real[0, h, 128 * k : 128 * (k + 1), :], turn_imag[0, h, 128 * k : 128 * (k + 1), :])
            for k, b in enumerate(blocks)
        ]
        put(sent.at[2, h], correct_x(blocks, padded_x, strength_x.at[0, h], block_right))
        field_out(2, h)

    both(correct_lines)

    arrived(vel_got, small_recv.at[0])

    def unpack_speed(i, carry):
        r = at(64 * i, 64, 64)
        x = vel_got[r, :]
        for d in range(2):
            for h in range(2):
                speed = spread(x, 2 * h + d)
                strength_y[d, h, r, :] = strength_of(speed, speeds[d])
                if d == 1:
                    real, imag = split_factors(speed, speeds[d], angular)
                    turn_real[1, h, r, :] = real
                    turn_imag[1, h, r, :] = imag
        return carry

    lax.fori_loop(0, 8, unpack_speed, 0)

    zeros = jnp.zeros((8, 128), F32)
    for h in range(2):
        padded_y[h, 0:8, :] = zeros
        padded_y[h, 520:528, :] = zeros

    def positions_x(h, row, column):
        line = me * 16 + 8 * h + row % 8
        index_x = row // 8 % 16 + 16 * (row // 128 * 32 + column)
        return index_x, line // 256 + 4 * (line % 256)

    phase_factors(phase_real.at[1], phase_imag.at[1], squares[1], positions_x)

    def fill_y(h):
        field_in(2, h)
        padded_y[h, 8:520, :] = got[2, h]

    both(fill_y)
    correct_y(padded_y, work_a, work_b, strength_y.at[0], block_left)

    def start_y(h):
        butterfly_forward(work_b.at[h], work_a.at[h], twist_y, h)
        operands[h] = left_operand(quarters(work_a.at[h]), 1)

    both(start_y)

    def send_y(h):
        put(sent.at[3, h], products_y(h))
        field_out(3, h)

    both(send_y)

    def image_y(i, carry):
        group_of = lanes() // 32
        r = at(64 * i, 64, 64)
        pieces = []
        for h in range(2):
            x = work_b[h, r, :]
            value = x * pltpu.roll(x, 96, 1)
            pieces.append(value - pltpu.roll(value, 64, 1))
        packed = jnp.where(group_of == 1, pltpu.roll(pieces[1], 32, 1), 0.0)
        img_sent[r, :] = jnp.where(group_of == 0, pieces[0], packed)
        return carry

    lax.fori_loop(0, 8, image_y, 0)
    exchange(img_sent, img_got, small_send.at[1], small_recv.at[1])

    def shift_x(h):
        field_in(3, h)
        blocks = outer_x(quarters(got.at[3, h]), left_x, twist_x, 1)
        blocks = right_product(right_x, blocks)
        blocks = [
            rotated(b, phase_real[1, h, 128 * k : 128 * (k + 1), :], phase_imag[1, h, 128 * k : 128 * (k + 1), :])
            for k, b in enumerate(blocks)
        ]
        blocks = inverse_inner_x(blocks, right_x)
        put(sent.at[4, h], outer_x(blocks, left_x, twist_x, -1))
        field_out(4, h)

    both(shift_x)

    def reduce_out(d):
        share(lambda g: part.at[d, at(2 * g, 2, 2)], shares.at[d], freq_send.at[1 + d], freq_recv.at[1 + d])

    def gather_out(d):
        arrived(shares.at[d], freq_recv.at[1 + d])
        total = shares[d, 0]
        for g in range(1, GROUPS):
            total = total + shares[d, g]
        summed[d] = total
        share(lambda g: summed.at[d], totals.at[d], freq_send.at[3 + d], freq_recv.at[3 + d])

    arrived(img_got, small_recv.at[1])

    def image_x(i, carry):
        group_of = lanes() // 32
        for low in range(2):
            a = 2 * i + low
            for h in range(2):
                result = jnp.zeros((8, 128), F32)
                for q in range(4):
                    x = img_got[at((q * 16 + a) * 8, 8, 8), :]
                    amount = 32 * (q - h) % 128
                    result = jnp.where(group_of == q, pltpu.roll(x, amount, 1) if amount else x, result)
                part[0, a, 8 * h : 8 * h + 8, :] = result
        return carry

    lax.fori_loop(0, 8, image_x, 0)
    reduce_out(0)

    for h in range(2):
        field_in(4, h)
        accumulate(part_in(4, h, got.at[4, h], -1), h)

    def finish_y(h):
        def split_y(x, r):
            return rotated(x, turn_real[1, h, r, :], turn_imag[1, h, r, :])

        butterfly_inverse(work_b.at[h], work_a.at[h], twist_y, h, split_y)
        padded_y[h, 8:520, :] = work_a[h]

    both(finish_y)
    correct_y(padded_y, work_a, sent.at[5], strength_y.at[1], block_left)

    def last_out(h):
        field_out(5, h)

    both(last_out)
    gather_out(0)

    def last_lines(h):
        field_in(5, h)
        blocks = correct_x(quarters(got.at[5, h]), padded_x, strength_x.at[1, h], block_right)
        whole = [regroup(blocks, g) for g in range(4)]
        image = whole[0] * whole[1] - whole[2] * whole[3]
        lines = at(8 * h, 8, 8)
        for a in range(16):
            r = slice(8 * a, 8 * a + 8)
            part[1, a, lines, :] = image[r]
            for g in range(4):
                out_ref[0, g % 2, g // 2, lines, 128 * a : 128 * (a + 1)] = whole[g][r]

    both(last_lines)
    reduce_out(1)
    gather_out(1)

    for d in range(2):
        arrived(totals.at[d], freq_recv.at[3 + d])
        for a in range(16):
            image_ref[d, :, 128 * a : 128 * (a + 1)] = totals[d, a // 2, a % 2]

    for k in range(6):
        for h in range(2):
            left_here(sent.at[k, h], send_sem.at[k, h])
    left_here(vel_sent, small_send.at[0])
    left_here(img_sent, small_send.at[1])
    shared_left(vel_all, freq_send.at[0])
    for d in range(2):
        shared_left(shares.at[d], freq_send.at[1 + d])
        shared_left(totals.at[d], freq_send.at[3 + d])


def scratch():
    def vmem(*shape, dtype=F32):
        return pltpu.VMEM(shape, dtype)

    def dma(*shape):
        return pltpu.SemaphoreType.DMA(shape)

    state = (2, 512, 128)
    return [
        vmem(1, 2, 2, 16, NX),
        vmem(2, 16, 256),
        vmem(1, 2, 128, 128),
        vmem(1, 2, 128, 128),
        vmem(128, 768, dtype=BF16),
        vmem(2, 512, 128),
        vmem(1536, 512, dtype=BF16),
        vmem(2, 256, 768, dtype=BF16),
        vmem(2, 2, 512, 128),
        vmem(6, *state),
        vmem(6, *state),
        vmem(*state),
        vmem(*state),
        vmem(2, 768, 512, dtype=BF16),
        vmem(768, 128),
        vmem(2, 528, 128),
        vmem(1536, 512, dtype=BF16),
        vmem(128, 768, dtype=BF16),
        vmem(2, *state),
        vmem(2, *state),
        vmem(2, *state),
        vmem(2, *state),
        vmem(2, *state),
        vmem(2, *state),
        vmem(GROUPS, 2, 16, 256),
        vmem(512, 128),
        vmem(512, 128),
        vmem(512, 128),
        vmem(512, 128),
        vmem(2, 16, 16, 128),
        vmem(2, GROUPS, 2, 16, 128),
        vmem(2, 2, 16, 128),
        vmem(2, GROUPS, 2, 16, 128),
        dma(6, 2),
        dma(6, 2),
        dma(2),
        dma(2),
        dma(5),
        dma(5),
        dma(9),
    ]


def body(wavefield, velocity, reference_velocity, frequencies, block_x, block_y):
    vmem, smem = pl.BlockSpec(memory_space=pltpu.VMEM), pl.BlockSpec(memory_space=pltpu.SMEM)
    anywhere = pl.BlockSpec(memory_space=pl.ANY)
    constants = [jnp.asarray(t) for t in tables()]
    call = pl.pallas_call(
        kernel,
        out_shape=(
            jax.ShapeDtypeStruct(wavefield.shape, F32),
            jax.ShapeDtypeStruct((2, 16, NX), F32),
        ),
        in_specs=[smem, smem] + [anywhere] * (4 + len(constants)),
        out_specs=(vmem, vmem),
        scratch_shapes=scratch(),
        compiler_params=pltpu.CompilerParams(
            collective_id=0, has_side_effects=True, vmem_limit_bytes=60 * 1024 * 1024
        ),
    )
    return call(reference_velocity, frequencies, wavefield, velocity, block_x, block_y, *constants)


def solution(mesh):
    in_specs = (
        P("freq", None, None, "slab", None),
        P(None, "slab", "freq"),
        P(),
        P("freq"),
        P("freq", None, None, None),
        P("freq", None, None, None),
    )
    out_specs = (P("freq", None, None, "slab", None), P(None, "slab", None))
    return jax.shard_map(body, mesh=mesh, in_specs=in_specs, out_specs=out_specs, check_vma=False)
```

time: 181 us -> 146 us (0.81)
  Pallas kernels: 167 us -> 141 us
  local copies, waits for them, and re-layouts: 12.2 us -> 2.62 us
    pallas_call x1, Pallas kernels: 167 us -> 141 us  [body(): call(reference_velocity, frequencies, wavefield, velocity, block_x, block...]
    unnamed x24 -> x4, local copies, waits for them, and re-layouts: 12.2 us -> 2.62 us
where the time goes in v2:
time: 146 us; the launch traced here: 145 us
  Pallas kernels  141 us (97%)
  local copies, waits for them, and re-layouts  2.62 us (2%)
    pallas_call x1, Pallas kernels, body(): call(reference_velocity, frequencies, wavefield, velocity, block_x, block...  141 us

profile of v2, /device:TPU:1, one launch (start us, length us, event | category | flops | bytes accessed | tf_op | source)
XLA Modules:
  0.0 144.7 jit_solution(17924066022909524247)
XLA Ops:
  1.3 140.8 %shard_map.122 = (f32[1,2,2,16,2048]{4,3,2,1,0:T(8,128)}, f32[2,16,2048]{2,1,0:T(8,128)}) custom-call(f32[2]{0:T(128)} %refv_ref.1, f32[1]{0:T(128)S(6)} %copy.15.freq_ref, f32[1,2,2,16,2048]{4,3,2,1,0:T(8,128)} %wave_hbm.1, f32[2,16,256]{2,1,0:T(8,128)} %vel_hbm.1, f32[1,2,128,128]{3,2,1,0:T(8,128)} %bx_hbm.1, f32[1,2,128,128]{3,2,1,0:T(8,128)} %by_hbm.1, ...), custom_call_target="tpu_custom_call" | custom-call | tf_op jit(solution)/shard_map/pallas_call | solution.py:816
  142.1 0.0 copy-start
  142.1 1.9 %copy.16 = f32[1,2,2,16,2048]{4,3,2,1,0:T(8,128)} copy(f32[1,2,2,16,2048]{4,3,2,1,0:T(8,128)} %get-tuple-element.4) | data formatting | bytes 1048576
  144.0 0.0 copy-done
  144.0 0.7 copy.17
Async XLA Ops:
  142.1 1.9 %copy-start = (f32[2,16,2048]{2,1,0:T(8,128)S(1)}, f32[2,16,2048]{2,1,0:T(8,128)}, u32[]{:S(2)}) copy-start(f32[2,16,2048]{2,1,0:T(8,128)} %get-tuple-element.5) | copy-start | bytes 786436

commit v3 on v2

--- a/solution.py
+++ b/solution.py
@@ -51,11 +51,11 @@
     left_y = np.stack(left_y)
     inner = np.arange(128)
     cos, sin = angle(inner[:, None] * inner[None, :], 128)
-    full = np.zeros((4, 2, 2, 32, 4, 2, 2, 32))
-    for field in range(2):
-        for c, d, block in ((0, 0, cos), (0, 1, sin), (1, 0, -sin), (1, 1, cos)):
-            full[:, c, field, :, :, d, field, :] = block.reshape(4, 32, 4, 32)
-    right_x = np.concatenate(split_table(full.reshape(512, 512)), 0)
+    full = np.zeros((2, 2, 2, 32, 2, 2, 2, 32))
+    for c, d, block in ((0, 0, cos), (0, 1, sin), (1, 0, -sin), (1, 1, cos)):
+        full[:, c, :, :, :, d, :, :] = block.reshape(2, 2, 32, 2, 2, 32)
+    high, low = split_table(full.reshape(256, 256))
+    right_x = np.concatenate([high, low, high], 0)
     quarter, outer, column = np.arange(4), np.arange(16), np.arange(32)
     position = quarter[:, None] * 32 + column[None, :]
     product = outer[None, :, None] * position[:, None, :]
@@ -113,8 +113,23 @@
 
 
 def right_product(table_ref, blocks):
-    highs, lows = zip(*[halves(x) for x in blocks])
-    return in_blocks(product(jnp.concatenate([*highs, *highs, *lows], 1), table_ref[...]))
+    odd = lanes() // 32 % 2 == 1
+    rows = blocks[0].shape[0]
+    operand = []
+    for p in range(2):
+        x, y = blocks[2 * p], blocks[2 * p + 1]
+        first = jnp.where(odd, pltpu.roll(y, 32, 1), x)
+        second = jnp.where(odd, y, pltpu.roll(x, 96, 1))
+        operand.append(halves(jnp.concatenate([first, second], 0)))
+    (high_0, low_0), (high_1, low_1) = operand
+    total = product(jnp.concatenate([high_0, high_1, high_0, high_1, low_0, low_1], 1), table_ref[...])
+    results = []
+    for p in range(2):
+        first = total[:rows, 128 * p : 128 * (p + 1)]
+        second = total[rows:, 128 * p : 128 * (p + 1)]
+        results.append(jnp.where(odd, pltpu.roll(second, 32, 1), first))
+        results.append(jnp.where(odd, second, pltpu.roll(first, 96, 1)))
+    return results
 
 
 def rotated(x, factor_real, factor_imag):
@@ -153,8 +168,8 @@
 
 
 def butterfly_forward(source, target, twist, h):
-    def step(i, carry):
-        rows = [at(128 * k + 32 * i, 32, 32) for k in range(4)]
+    for i in range(4):
+        rows = [slice(128 * k + 32 * i, 128 * k + 32 * i + 32) for k in range(4)]
         x0, x1, x2, x3 = [source[r, :] for r in rows]
         even, odd = x0 + x2, x1 + x3
         minus, spun = x0 - x2, turn(x1 - x3)
@@ -164,14 +179,11 @@
             if k > 0:
                 value = rotated(value, twist[0, h, r, :], twist[1, h, r, :])
             target[r, :] = value
-        return carry
-
-    lax.fori_loop(0, 4, step, 0)
 
 
 def butterfly_inverse(source, target, twist, h, finish):
-    def step(i, carry):
-        rows = [at(128 * k + 32 * i, 32, 32) for k in range(4)]
+    for i in range(4):
+        rows = [slice(128 * k + 32 * i, 128 * k + 32 * i + 32) for k in range(4)]
         x0, x1, x2, x3 = [source[r, :] for r in rows]
         x1, x2, x3 = [
             rotated_back(x, twist[0, h, r, :], twist[1, h, r, :])
@@ -182,9 +194,6 @@
         results = [even + odd, minus + spun, even - odd, minus - spun]
         for value, r in zip(results, rows):
             target[r, :] = finish(value, r)
-        return carry
-
-    lax.fori_loop(0, 4, step, 0)
 
 
 def series(square, first):
@@ -304,19 +313,17 @@
         for place, value in ((k, high), (2 + k, high), (4 + k, low)):
             left_ref[:, 128 * place : 128 * (place + 1)] = value
     real, imag = bx_ref[0, 0].T, bx_ref[0, 1].T
-    zero = jnp.zeros_like(real)
+    front = lanes() < 64
     for c in range(2):
-        pair = (real, imag) if c == 0 else (-imag, real)
-        for field in range(2):
-            blocks = [zero] * 4
-            blocks[field], blocks[2 + field] = pair
-            for quarter in range(4):
-                high, low = halves(regroup(blocks, quarter))
-                columns = slice(128 * quarter, 128 * (quarter + 1))
-                for q in range(4):
-                    base = 128 * q + 64 * c + 32 * field
-                    for offset, value in ((0, high), (512, low), (1024, high)):
-                        right_ref[offset + base : offset + base + 32, columns] = value[32 * q : 32 * q + 32]
+        x, y = (real, imag) if c == 0 else (-imag, real)
+        pairs = (jnp.where(front, x, pltpu.roll(y, 64, 1)), jnp.where(front, pltpu.roll(x, 64, 1), y))
+        for p, pair in enumerate(pairs):
+            high, low = halves(pair)
+            columns = slice(128 * p, 128 * (p + 1))
+            for q in range(4):
+                base = 128 * (q // 2) + 64 * c + 32 * (q % 2)
+                for offset, value in ((0, high), (256, low), (512, high)):
+                    right_ref[offset + base : offset + base + 32, columns] = value[32 * q : 32 * q + 32]
 
 
 def kernel(
@@ -382,7 +389,7 @@
         (wave_hbm, wave_ref),
         (left_x_hbm, left_x),
         (twist_x_hbm, twist_x),
-        (right_x_hbm, right_x.at[0:1024, :]),
+        (right_x_hbm, right_x),
         (vel_hbm, vel_ref),
         (left_y_hbm, left_y),
         (twist_y_hbm, twist_y),
@@ -410,18 +417,19 @@
         own = at(me * HALF, HALF, HALF)
 
         def step(i, carry):
-            other = lax.rem(me + i * STRIDE, SLABS)
-            pltpu.make_async_remote_copy(
-                src_ref=source.at[at(other * HALF, HALF, HALF), :],
-                dst_ref=landing.at[own, :],
-                send_sem=send,
-                recv_sem=recv,
-                device_id=(group, other),
-                device_id_type=MESH,
-            ).start()
+            for k in range(1, 4):
+                other = lax.rem(me + (3 * i + k) * STRIDE, SLABS)
+                pltpu.make_async_remote_copy(
+                    src_ref=source.at[at(other * HALF, HALF, HALF), :],
+                    dst_ref=landing.at[own, :],
+                    send_sem=send,
+                    recv_sem=recv,
+                    device_id=(group, other),
+                    device_id_type=MESH,
+                ).start()
             return carry
 
-        lax.fori_loop(1, SLABS, step, 0)
+        lax.fori_loop(0, (SLABS - 1) // 3, step, 0)
         pltpu.make_async_copy(source.at[own, :], landing.at[own, :], recv).start()
 
     def arrived(landing, recv):
@@ -479,19 +487,14 @@
     loads[3].wait()
     loads[4].wait()
 
-    def repeat_table(i, carry):
-        right_x[at(1024 + 128 * i, 128, 128), :] = right_x[at(128 * i, 128, 128), :]
-        return carry
-
-    lax.fori_loop(0, 4, repeat_table, 0)
     pl.semaphore_wait(barrier, SLABS - 1 + GROUPS - 1)
 
     def send_x(h):
         put(sent.at[0, h], right_product(right_x, quarters(work_a.at[h])))
         field_out(0, h)
 
+    share(lambda g: vel_ref, vel_all, freq_send.at[0], freq_recv.at[0])
     both(send_x)
-    share(lambda g: vel_ref, vel_all, freq_send.at[0], freq_recv.at[0])
 
     angular = jnp.full((1, 128), freq_ref[0], F32) * (2.0 * math.pi)
     speeds = [jnp.full((1, 128), refv_ref[d], F32) for d in range(2)]
@@ -503,45 +506,6 @@
         return index_x, row // 128 + 4 * (16 * (rest // 8) + 8 * h + rest % 8)
 
     phase_factors(phase_real.at[0], phase_imag.at[0], squares[0], positions_y)
-    loads[5].wait()
-    loads[6].wait()
-
-    def part_in(k, h, source, direction):
-        operand = left_operand(quarters(source), direction)
-        return in_blocks(product(left_y[h], operand))
-
-    def accumulate(parts, h):
-        for k, x in enumerate(parts):
-            for m in range(2):
-                r = slice(128 * k, 128 * (k + 1))
-                value = x[128 * m : 128 * (m + 1)]
-                work_b[m, r, :] = value if h == 0 else work_b[m, r, :] + value
-
-    def products_y(h):
-        rows = at(128 * h, 128, 128)
-        total = product(left_y[0, rows, :], operands[0]) + product(left_y[1, rows, :], operands[1])
-        return in_blocks(total)
-
-    for h in range(2):
-        field_in(0, h)
-        butterfly_forward(got.at[0, h], work_a.at[h], twist_y, h)
-        accumulate(part_in(0, h, work_a.at[h], 1), h)
-
-    def shift_y(m):
-        blocks = [
-            rotated(b, phase_real[0, m, 128 * k : 128 * (k + 1), :], phase_imag[0, m, 128 * k : 128 * (k + 1), :])
-            for k, b in enumerate(quarters(work_b.at[m]))
-        ]
-        operands[m] = left_operand(blocks, -1)
-
-    both(shift_y)
-
-    def back_y(h):
-        put(work_a.at[h], products_y(h))
-        butterfly_inverse(work_a.at[h], sent.at[1, h], twist_y, h, lambda x, r: x)
-        field_out(1, h)
-
-    both(back_y)
 
     arrived(vel_all, freq_recv.at[0])
 
@@ -569,6 +533,46 @@
 
     lax.fori_loop(0, GROUPS, pack_speed, 0)
     exchange(vel_sent, vel_got, small_send.at[0], small_recv.at[0])
+    loads[5].wait()
+    loads[6].wait()
+
+    def part_in(k, h, source, direction):
+        operand = left_operand(quarters(source), direction)
+        return in_blocks(product(left_y[h], operand))
+
+    def accumulate(parts, h):
+        for k, x in enumerate(parts):
+            for m in range(2):
+                r = slice(128 * k, 128 * (k + 1))
+                value = x[128 * m : 128 * (m + 1)]
+                work_b[m, r, :] = value if h == 0 else work_b[m, r, :] + value
+
+    def products_y(h):
+        rows = at(128 * h, 128, 128)
+        total = product(left_y[0, rows, :], operands[0]) + product(left_y[1, rows, :], operands[1])
+        return in_blocks(total)
+
+    for h in range(2):
+        field_in(0, h)
+        butterfly_forward(got.at[0, h], work_a.at[h], twist_y, h)
+        accumulate(part_in(0, h, work_a.at[h], 1), h)
+
+    def shift_y(m):
+        blocks = [
+            rotated(b, phase_real[0, m, 128 * k : 128 * (k + 1), :], phase_imag[0, m, 128 * k : 128 * (k + 1), :])
+            for k, b in enumerate(quarters(work_b.at[m]))
+        ]
+        operands[m] = left_operand(blocks, -1)
+
+    both(shift_y)
+
+    def back_y(h):
+        put(work_a.at[h], products_y(h))
+        butterfly_inverse(work_a.at[h], sent.at[1, h], twist_y, h, lambda x, r: x)
+        field_out(1, h)
+
+    both(back_y)
+
     loads[7].wait()
     loads[8].wait()
     build_blocks(bx_ref, by_ref, block_right, block_left)
@@ -647,8 +651,6 @@
         return carry
 
     lax.fori_loop(0, 8, image_y, 0)
-    exchange(img_sent, img_got, small_send.at[1], small_recv.at[1])
-
     def shift_x(h):
         field_in(3, h)
         blocks = outer_x(quarters(got.at[3, h]), left_x, twist_x, 1)
@@ -663,16 +665,39 @@
 
     both(shift_x)
 
-    def reduce_out(d):
-        share(lambda g: part.at[d, at(2 * g, 2, 2)], shares.at[d], freq_send.at[1 + d], freq_recv.at[1 + d])
-
-    def gather_out(d):
-        arrived(shares.at[d], freq_recv.at[1 + d])
-        total = shares[d, 0]
+    for h in range(2):
+        field_in(4, h)
+        accumulate(part_in(4, h, got.at[4, h], -1), h)
+        if h == 0:
+            exchange(img_sent, img_got, small_send.at[1], small_recv.at[1])
+
+    def finish_y(h):
+        def split_y(x, r):
+            return rotated(x, turn_real[1, h, r, :], turn_imag[1, h, r, :])
+
+        butterfly_inverse(work_b.at[h], work_a.at[h], twist_y, h, split_y)
+        padded_y[h, 8:520, :] = work_a[h]
+
+    both(finish_y)
+    correct_y(padded_y, work_a, sent.at[5], strength_y.at[1], block_left)
+
+    def last_out(h):
+        field_out(5, h)
+
+    both(last_out)
+
+    def reduce_out(d, h):
+        k = 1 + 2 * d + h
+        share(lambda g: part.at[d, h, at(2 * g, 2, 2)], shares.at[d, h], freq_send.at[k], freq_recv.at[k])
+
+    def gather_out(d, h):
+        arrived(shares.at[d, h], freq_recv.at[1 + 2 * d + h])
+        total = shares[d, h, 0]
         for g in range(1, GROUPS):
-            total = total + shares[d, g]
-        summed[d] = total
-        share(lambda g: summed.at[d], totals.at[d], freq_send.at[3 + d], freq_recv.at[3 + d])
+            total = total + shares[d, h, g]
+        summed[d, h] = total
+        k = 5 + 2 * d + h
+        share(lambda g: summed.at[d, h], totals.at[d, h], freq_send.at[k], freq_recv.at[k])
 
     arrived(img_got, small_recv.at[1])
 
@@ -686,52 +711,38 @@
                     x = img_got[at((q * 16 + a) * 8, 8, 8), :]
                     amount = 32 * (q - h) % 128
                     result = jnp.where(group_of == q, pltpu.roll(x, amount, 1) if amount else x, result)
-                part[0, a, 8 * h : 8 * h + 8, :] = result
+                part[0, h, a] = result
         return carry
 
     lax.fori_loop(0, 8, image_x, 0)
-    reduce_out(0)
-
     for h in range(2):
-        field_in(4, h)
-        accumulate(part_in(4, h, got.at[4, h], -1), h)
-
-    def finish_y(h):
-        def split_y(x, r):
-            return rotated(x, turn_real[1, h, r, :], turn_imag[1, h, r, :])
-
-        butterfly_inverse(work_b.at[h], work_a.at[h], twist_y, h, split_y)
-        padded_y[h, 8:520, :] = work_a[h]
-
-    both(finish_y)
-    correct_y(padded_y, work_a, sent.at[5], strength_y.at[1], block_left)
-
-    def last_out(h):
-        field_out(5, h)
-
-    both(last_out)
-    gather_out(0)
+        reduce_out(0, h)
 
     def last_lines(h):
         field_in(5, h)
         blocks = correct_x(quarters(got.at[5, h]), padded_x, strength_x.at[1, h], block_right)
         whole = [regroup(blocks, g) for g in range(4)]
         image = whole[0] * whole[1] - whole[2] * whole[3]
-        lines = at(8 * h, 8, 8)
+        lines = slice(8 * h, 8 * h + 8)
         for a in range(16):
-            r = slice(8 * a, 8 * a + 8)
-            part[1, a, lines, :] = image[r]
+            part[1, h, a] = image[8 * a : 8 * a + 8]
+        reduce_out(1, h)
+        for a in range(16):
             for g in range(4):
-                out_ref[0, g % 2, g // 2, lines, 128 * a : 128 * (a + 1)] = whole[g][r]
-
-    both(last_lines)
-    reduce_out(1)
-    gather_out(1)
+                out_ref[0, g % 2, g // 2, lines, 128 * a : 128 * (a + 1)] = whole[g][8 * a : 8 * a + 8]
+
+    last_lines(0)
+    for h in range(2):
+        gather_out(0, h)
+    last_lines(1)
+    for h in range(2):
+        gather_out(1, h)
 
     for d in range(2):
-        arrived(totals.at[d], freq_recv.at[3 + d])
-        for a in range(16):
-            image_ref[d, :, 128 * a : 128 * (a + 1)] = totals[d, a // 2, a % 2]
+        for h in range(2):
+            arrived(totals.at[d, h], freq_recv.at[5 + 2 * d + h])
+            for a in range(16):
+                image_ref[d, 8 * h : 8 * h + 8, 128 * a : 128 * (a + 1)] = totals[d, h, a // 2, a % 2]
 
     for k in range(6):
         for h in range(2):
@@ -740,8 +751,9 @@
     left_here(img_sent, small_send.at[1])
     shared_left(vel_all, freq_send.at[0])
     for d in range(2):
-        shared_left(shares.at[d], freq_send.at[1 + d])
-        shared_left(totals.at[d], freq_send.at[3 + d])
+        for h in range(2):
+            shared_left(shares.at[d, h], freq_send.at[1 + 2 * d + h])
+            shared_left(totals.at[d, h], freq_send.at[5 + 2 * d + h])
 
 
 def scratch():
@@ -759,7 +771,7 @@
         vmem(1, 2, 128, 128),
         vmem(128, 768, dtype=BF16),
         vmem(2, 512, 128),
-        vmem(1536, 512, dtype=BF16),
+        vmem(768, 256, dtype=BF16),
         vmem(2, 256, 768, dtype=BF16),
         vmem(2, 2, 512, 128),
         vmem(6, *state),
@@ -769,7 +781,7 @@
         vmem(2, 768, 512, dtype=BF16),
         vmem(768, 128),
         vmem(2, 528, 128),
-        vmem(1536, 512, dtype=BF16),
+        vmem(768, 256, dtype=BF16),
         vmem(128, 768, dtype=BF16),
         vmem(2, *state),
         vmem(2, *state),
@@ -782,16 +794,16 @@
         vmem(512, 128),
         vmem(512, 128),
         vmem(512, 128),
-        vmem(2, 16, 16, 128),
-        vmem(2, GROUPS, 2, 16, 128),
-        vmem(2, 2, 16, 128),
-        vmem(2, GROUPS, 2, 16, 128),
+        vmem(2, 2, 16, 8, 128),
+        vmem(2, 2, GROUPS, 2, 8, 128),
+        vmem(2, 2, 2, 8, 128),
+        vmem(2, 2, GROUPS, 2, 8, 128),
         dma(6, 2),
         dma(6, 2),
         dma(2),
         dma(2),
-        dma(5),
-        dma(5),
+        dma(9),
+        dma(9),
         dma(9),
     ]
 

time: 146 us -> 144 us (0.986)
  no operation moved by 1% of the time
where the time goes in v3:
time: 144 us
  Pallas kernels  140 us (97%)
  local copies, waits for them, and re-layouts  2.62 us (2%)
    pallas_call x1, Pallas kernels, body(): call(reference_velocity, frequencies, wavefield, velocity, block_x, block...  140 us

profile of v3, /device:TPU:1, one launch (start us, length us, event | category | flops | bytes accessed | tf_op | source)
XLA Modules:
  0.0 143.8 jit_solution(9059781700465308309)
XLA Ops:
  1.3 139.9 %shard_map.122 = (f32[1,2,2,16,2048]{4,3,2,1,0:T(8,128)}, f32[2,16,2048]{2,1,0:T(8,128)}) custom-call(f32[2]{0:T(128)} %refv_ref.1, f32[1]{0:T(128)S(6)} %copy.15.freq_ref, f32[1,2,2,16,2048]{4,3,2,1,0:T(8,128)} %wave_hbm.1, f32[2,16,256]{2,1,0:T(8,128)} %vel_hbm.1, f32[1,2,128,128]{3,2,1,0:T(8,128)} %bx_hbm.1, f32[1,2,128,128]{3,2,1,0:T(8,128)} %by_hbm.1, ...), custom_call_target="tpu_custom_call" | custom-call | tf_op jit(solution)/shard_map/pallas_call | solution.py:828
  141.2 0.0 copy-start
  141.2 1.9 %copy.16 = f32[1,2,2,16,2048]{4,3,2,1,0:T(8,128)} copy(f32[1,2,2,16,2048]{4,3,2,1,0:T(8,128)} %get-tuple-element.4) | data formatting | bytes 1048576
  143.1 0.0 copy-done
  143.1 0.7 copy.17
Async XLA Ops:
  141.2 1.9 %copy-start = (f32[2,16,2048]{2,1,0:T(8,128)S(1)}, f32[2,16,2048]{2,1,0:T(8,128)}, u32[]{:S(2)}) copy-start(f32[2,16,2048]{2,1,0:T(8,128)} %get-tuple-element.5) | copy-start | bytes 786436
